TPU v7x, 32 devices: a whole 2x2x4 slice. The times are simulated.
32 devices in a mesh: front: 8 (over y, x, core), enc: 4 (over z).
Axes of the slice: x: 2, y: 2, z: 4, core: 2. Of those that a mesh axis runs over, the one named last changes fastest.
Arguments:
- spectra: bfloat16 [1024, 56, 80], P('front'), may hold values from -6 to 6
- sub_weight: bfloat16 [640, 1024], P(None, 'enc'), may hold values from -0.25 to 0.25
- sub_bias: bfloat16 [1024], P('enc'), may hold values from -4 to 4
- key_cache: bfloat16 [1024, 70, 1024], P('front', None, 'enc'), may hold values from -1000 to 1000
- value_cache: bfloat16 [1024, 70, 1024], P('front', None, 'enc'), may hold values from -6 to 6
- conv_cache: bfloat16 [1024, 8, 1024], P('front', None, 'enc'), may hold values from -6 to 6
- new_slot: int32 [1024], P('front'), may hold values from 0 to 1023, as said below
- old_slot: int32 [1024], P('front'), may hold values from 0 to 1023, as said below
- valid_new: int32 [1024], P('front'), may hold values from 1 to 7
- cache_fill: int32 [1024], P('front'), may hold values from 0 to 70
- ln1_gain: float32 [1024], replicated, may hold values from 0.5 to 1.5
- w_query: bfloat16 [1024, 1024], P(None, 'enc'), may hold values from -0.1875 to 0.1875
- w_key: bfloat16 [1024, 1024], P(None, 'enc'), may hold values from -0.1875 to 0.1875
- w_value: bfloat16 [1024, 1024], P(None, 'enc'), may hold values from -0.1875 to 0.1875
- w_attn_out: bfloat16 [1024, 1024], P('enc'), may hold values from -0.1875 to 0.1875
- ln2_gain: float32 [1024], replicated, may hold values from 0.5 to 1.5
- w_glu_value: bfloat16 [1024, 1024], P(None, 'enc'), may hold values from -0.1875 to 0.1875
- w_glu_gate: bfloat16 [1024, 1024], P(None, 'enc'), may hold values from -0.1875 to 0.1875
- depth_kernel: float32 [9, 1024], P(None, 'enc'), may hold values from -2 to 2
- norm_scale: float32 [1024], P('enc'), may hold values from 0.1 to 1.9
- norm_shift: float32 [1024], P('enc'), may hold values from -3 to 3
- w_conv_out: bfloat16 [1024, 1024], P('enc'), may hold values from -0.1875 to 0.1875
Outputs:
- encoded: bfloat16 [1024, 7, 1024], P('front', None, 'enc')
- key_out: bfloat16 [1024, 70, 1024], P('front', None, 'enc')
- value_out: bfloat16 [1024, 70, 1024], P('front', None, 'enc')
- conv_out: bfloat16 [1024, 8, 1024], P('front', None, 'enc')
Inputs may be any that keep to these rules, and one draw needn't show every extreme that they name: `new_slot`: A permutation of the stream slots. Device f of front holds old slots and new slots f * 128 to (f + 1) * 128 - 1; a stream that stays on its device keeps its slot; each device hands at most 2 streams to any other device, to at most 4 other devices, and receives as many streams as it hands away. `old_slot`: the inverse permutation of new_slot.
All inputs are finite; a program needn't handle non-finite values.
Results may differ from a plain program's by a relative error of at most 0.0095.
Values may be sent and summed in bfloat16 or wider, within the bound.
A program may use at most 128 MiB of HBM per device.

v0:
```python
import functools
import math

import jax
import jax.numpy as jnp
from jax import lax
from jax.experimental import pallas as pl
from jax.experimental.pallas import tpu as pltpu
from jax.sharding import PartitionSpec as P

KERNEL = 9
SUB = 8
FRAMES = 7
CACHE = 70
TOTAL = CACHE + FRAMES
CAP = 2
HEAD = 128
CONV_CACHE = 8
GROUP = 16
VMEM_LIMIT = 56 * 1024 * 1024

masked_score = -1e30
BF = jnp.bfloat16
F32 = jnp.float32


def mm(a, b):
    return jnp.dot(a, b, preferred_element_type=F32)


def layer_norm(values_in, gain):
    average = jnp.mean(values_in, axis=-1, keepdims=True)
    centered = values_in - average
    spread = jnp.mean(centered * centered, axis=-1, keepdims=True)
    return centered * lax.rsqrt(spread + 1e-05) * gain


def send_slots(new_slot, own_index, peer_count, stream_count):
    target = new_slot // stream_count
    leaving = target != own_index
    index = jnp.arange(stream_count, dtype=jnp.int32)
    earlier = (target[None, :] == target[:, None]) & (index[None, :] < index[:, None])
    position = jnp.sum(earlier.astype(jnp.int32), axis=1)
    bucket = jnp.where(leaving, target * CAP + position, peer_count * CAP)
    return bucket[None, :] == jnp.arange(peer_count * CAP, dtype=jnp.int32)[:, None]


def arrival_slots(old_slot, own_index, slots):
    stream_count = old_slot.shape[0]
    source = old_slot // stream_count
    staying = source == own_index
    earlier = (source[None, :] == source[:, None]) & (old_slot[None, :] < old_slot[:, None])
    position = jnp.sum(earlier.astype(jnp.int32), axis=1)
    arrival = jnp.where(staying, slots, source * CAP + position)
    return arrival, staying


def shift_rows(block, masks):
    for mask, step in zip(masks, (1, 2, 4)):
        block = jnp.where(mask[None], block[step:], block[:-step])
    return block


def project_kernel(x_ref, sw_ref, sb_ref, gain_ref, wq_ref, wk_ref, wv_ref, in_ref, q_ref, k_ref, v_ref):
    x = x_ref[0]
    parts = []
    for g in range(sw_ref.shape[0]):
        part = lax.dot_general(x, sw_ref[g], (((0,), (0,)), ((), ())), preferred_element_type=F32)
        parts.append(part)
    inputs = (jnp.concatenate(parts, axis=1) + sb_ref[...]).astype(BF)
    in_ref[0] = inputs
    normed = layer_norm(inputs.astype(F32), gain_ref[...]).astype(BF)
    q_ref[0] = mm(normed, wq_ref[...]).astype(BF)
    k_ref[0] = mm(normed, wk_ref[...]).astype(BF)
    v_ref[0] = mm(normed, wv_ref[...]).astype(BF)


def project(x, sw, sb, gain, wq, wk, wv):
    frames, depth, streams = x.shape
    width = wq.shape[0]
    local = wq.shape[1]
    whole = lambda shape: pl.BlockSpec(shape, lambda t: (0,) * len(shape))
    row = lambda w: pl.BlockSpec((1, streams, w), lambda t: (t, 0, 0))
    return pl.pallas_call(
        project_kernel,
        grid=(frames,),
        in_specs=[
            pl.BlockSpec((1, depth, streams), lambda t: (t, 0, 0)),
            whole(sw.shape),
            whole(sb.shape),
            whole(gain.shape),
            whole(wq.shape),
            whole(wk.shape),
            whole(wv.shape),
        ],
        out_specs=[row(width), row(local), row(local), row(local)],
        out_shape=[jax.ShapeDtypeStruct((frames, streams, width), BF)]
        + [jax.ShapeDtypeStruct((frames, streams, local), BF)] * 3,
        compiler_params=pltpu.CompilerParams(vmem_limit_bytes=VMEM_LIMIT),
        name="project",
    )(x, sw, sb, gain, wq, wk, wv)


def attend_kernel(
    has_ref, q_ref, kn_ref, vn_ref, kc_ref, vc_ref, kr_ref, vr_ref, pick_ref, bits_ref, stay_ref,
    colbias_ref, match_ref, ctx_ref, ko_ref, vo_ref, kall, vall,
):
    group = pl.program_id(0)
    local = q_ref.shape[2]
    slots = kr_ref.shape[1]
    span = pick_ref.shape[2] // slots
    kall[0:CACHE] = kc_ref[...]
    vall[0:CACHE] = vc_ref[...]

    @pl.when(has_ref[group] > 0)
    def _():
        stay = (stay_ref[...] > 0.5)[None]
        for first in range(0, CACHE, span):
            count = min(span, CACHE - first)
            pick = pick_ref[0, : count * GROUP, : count * slots]
            for rec, dest in ((kr_ref, kall), (vr_ref, vall)):
                rows = rec[first : first + count].reshape(count * slots, local)
                fetched = mm(pick, rows).astype(BF).reshape(count, GROUP, local)
                dest[first : first + count] = jnp.where(stay, dest[first : first + count], fetched)

    kall[CACHE:TOTAL] = kn_ref[...]
    vall[CACHE:TOTAL] = vn_ref[...]
    bias = match_ref[...] + colbias_ref[0]
    for h in range(local // HEAD):
        lanes = slice(h * HEAD, (h + 1) * HEAD)
        qh = q_ref[:, :, lanes].reshape(FRAMES * GROUP, HEAD)
        kh = kall[:, :, lanes].reshape(TOTAL * GROUP, HEAD)
        vh = vall[:, :, lanes].reshape(TOTAL * GROUP, HEAD)
        scores = lax.dot_general(qh, kh, (((1,), (1,)), ((), ())), preferred_element_type=F32)
        scores = scores * (1.0 / math.sqrt(HEAD)) + bias
        peak = jnp.max(scores, axis=-1, keepdims=True)
        expo = jnp.exp(scores - peak)
        weights = (expo * (1.0 / jnp.sum(expo, axis=-1, keepdims=True))).astype(BF)
        ctx_ref[:, :, lanes] = mm(weights, vh).astype(BF).reshape(FRAMES, GROUP, HEAD)
    masks = [bits_ref[b] > 0.5 for b in range(3)]
    step = 10
    for src, dst in ((kall, ko_ref), (vall, vo_ref)):
        for first in range(0, CACHE, step):
            dst[first : first + step] = shift_rows(src[first : first + step + FRAMES], masks)


def attend(has, q, kn, vn, kc, vc, kr, vr, pick, bits, stay, colbias, match):
    streams, local = q.shape[1:]
    groups = streams // GROUP
    slots = kr.shape[1]
    block = lambda n: pl.BlockSpec((n, GROUP, local), lambda g, *_: (0, g, 0))
    whole = lambda shape: pl.BlockSpec(shape, lambda g, *_: (0,) * len(shape))
    return pl.pallas_call(
        attend_kernel,
        grid_spec=pltpu.PrefetchScalarGridSpec(
            num_scalar_prefetch=1,
            grid=(groups,),
            in_specs=[
                block(FRAMES), block(FRAMES), block(FRAMES), block(CACHE), block(CACHE),
                whole(kr.shape), whole(vr.shape),
                pl.BlockSpec((1,) + pick.shape[1:], lambda g, *_: (g, 0, 0)),
                block(3),
                pl.BlockSpec((GROUP, local), lambda g, *_: (g, 0)),
                pl.BlockSpec((1, 1, TOTAL * GROUP), lambda g, *_: (g, 0, 0)),
                whole(match.shape),
            ],
            out_specs=[block(FRAMES), block(CACHE), block(CACHE)],
            scratch_shapes=[pltpu.VMEM((TOTAL, GROUP, local), BF)] * 2,
        ),
        out_shape=[
            jax.ShapeDtypeStruct((FRAMES, streams, local), BF),
            jax.ShapeDtypeStruct((CACHE, streams, local), BF),
            jax.ShapeDtypeStruct((CACHE, streams, local), BF),
        ],
        compiler_params=pltpu.CompilerParams(vmem_limit_bytes=VMEM_LIMIT),
        cost_estimate=pl.CostEstimate(flops=1200000000, bytes_accessed=20000000, transcendentals=2500000),
        name="attend",
    )(has, q, kn, vn, kc, vc, kr, vr, pick, bits, stay, colbias, match)


def convolve_kernel(
    ctx_ref, in_ref, wo_ref, gain_ref, wv_ref, wg_ref, conv_ref, bits_ref, dk_ref, scale_ref, bias_ref,
    mid_ref, act_ref, co_ref, conv_all,
):
    parts, frames, streams, local = ctx_ref.shape
    width = in_ref.shape[2]
    rows = frames * streams
    attended = jnp.zeros((rows, width), F32)
    for g in range(parts):
        share = mm(ctx_ref[g].reshape(rows, local), wo_ref[g * local : (g + 1) * local])
        attended = attended + share.astype(BF).astype(F32)
    middle = (in_ref[...].reshape(rows, width).astype(F32) + attended).astype(BF)
    mid_ref[...] = middle.reshape(frames, streams, width)
    normed = layer_norm(middle.astype(F32), gain_ref[...]).astype(BF)
    gated = (mm(normed, wv_ref[...]) * jax.nn.sigmoid(mm(normed, wg_ref[...]))).astype(BF)
    conv_all[0:CONV_CACHE] = conv_ref[...]
    conv_all[CONV_CACHE:] = gated.reshape(frames, streams, local)
    taps = [dk_ref[k : k + 1, :] for k in range(KERNEL)]
    for t in range(frames):
        total = jnp.zeros((streams, local), F32)
        for k in range(KERNEL):
            total = total + taps[k] * conv_all[t + k].astype(F32)
        shaped = total * scale_ref[...] + bias_ref[...]
        act_ref[t] = (shaped * jax.nn.sigmoid(shaped)).astype(BF)
    co_ref[...] = shift_rows(conv_all[...], [bits_ref[b] > 0.5 for b in range(3)])


def convolve(ctx, inputs, wo, gain, wv, wg, conv, bits, dk, scale, bias):
    parts, frames, streams, local = ctx.shape
    width = inputs.shape[2]
    size = min(64, streams)
    whole = lambda shape: pl.BlockSpec(shape, lambda g: (0,) * len(shape))
    block = lambda n, w: pl.BlockSpec((n, size, w), lambda g: (0, g, 0))
    return pl.pallas_call(
        convolve_kernel,
        grid=(streams // size,),
        in_specs=[
            pl.BlockSpec((parts, frames, size, local), lambda g: (0, 0, g, 0)),
            block(frames, width),
            whole(wo.shape), whole(gain.shape), whole(wv.shape), whole(wg.shape),
            block(CONV_CACHE, local), block(3, local),
            whole(dk.shape), whole(scale.shape), whole(bias.shape),
        ],
        out_specs=[block(frames, width), block(frames, local), block(CONV_CACHE, local)],
        out_shape=[
            jax.ShapeDtypeStruct((frames, streams, width), BF),
            jax.ShapeDtypeStruct((frames, streams, local), BF),
            jax.ShapeDtypeStruct((CONV_CACHE, streams, local), BF),
        ],
        scratch_shapes=[pltpu.VMEM((CONV_CACHE + frames, size, local), BF)],
        compiler_params=pltpu.CompilerParams(vmem_limit_bytes=VMEM_LIMIT),
        name="convolve",
    )(ctx, inputs, wo, gain, wv, wg, conv, bits, dk, scale, bias)


def finish_kernel(me_ref, act_ref, wc_ref, mid_ref, valid_ref, out_ref):
    parts, frames, streams, local = act_ref.shape
    rows = frames * streams
    total = jnp.zeros((rows, local), F32)
    for g in range(parts):
        share = mm(act_ref[g].reshape(rows, local), wc_ref[g * local : (g + 1) * local])
        total = total + share.astype(BF).astype(F32)
    total = total + mid_ref[...].reshape(rows, local).astype(F32)
    total = total.reshape(frames, streams, local)
    for t in range(frames):
        out_ref[t] = jnp.where(valid_ref[...] > t + 0.5, total[t], 0.0).astype(BF)


def finish(me, act, wc, middle, valid_wide):
    parts, frames, streams, local = act.shape
    size = min(64, streams)
    return pl.pallas_call(
        finish_kernel,
        grid_spec=pltpu.PrefetchScalarGridSpec(
            num_scalar_prefetch=1,
            grid=(streams // size,),
            in_specs=[
                pl.BlockSpec((parts, frames, size, local), lambda g, m: (0, 0, g, 0)),
                pl.BlockSpec(wc.shape, lambda g, m: (0, 0)),
                pl.BlockSpec((frames, size, local), lambda g, m: (0, g, m[0])),
                pl.BlockSpec((size, local), lambda g, m: (g, 0)),
            ],
            out_specs=pl.BlockSpec((frames, size, local), lambda g, m: (0, g, 0)),
        ),
        out_shape=jax.ShapeDtypeStruct((frames, streams, local), BF),
        compiler_params=pltpu.CompilerParams(vmem_limit_bytes=VMEM_LIMIT),
        name="finish",
    )(me, act, wc, middle, valid_wide)


def on_device(
    spectra,
    sub_weight,
    sub_bias,
    key_cache,
    value_cache,
    conv_cache,
    new_slot,
    old_slot,
    valid_new,
    cache_fill,
    ln1_gain,
    w_query,
    w_key,
    w_value,
    w_attn_out,
    ln2_gain,
    w_glu_value,
    w_glu_gate,
    depth_kernel,
    norm_scale,
    norm_shift,
    w_conv_out,
):
    peer_count = lax.axis_size("front")
    own_index = lax.axis_index("front")
    member = lax.axis_index("enc")
    streams = spectra.shape[0]
    local = w_query.shape[1]
    slots = peer_count * CAP
    mels = spectra.shape[2]

    sub_full = lax.all_gather(sub_weight, "enc")
    bias_full = lax.all_gather(sub_bias, "enc", tiled=True).astype(F32)[None]
    attn_full = lax.all_gather(w_attn_out, "enc", tiled=True)
    conv_cols = lax.all_to_all(w_conv_out, "enc", split_axis=1, concat_axis=0, tiled=True)

    leaving = send_slots(new_slot, own_index, peer_count, streams).astype(BF)
    arrival, staying = arrival_slots(old_slot, own_index, slots)
    arriving = (arrival[:, None] == jnp.arange(slots, dtype=jnp.int32)[None, :]).astype(BF)

    x = spectra.transpose(1, 2, 0).reshape(FRAMES * SUB * mels, streams)
    x_send = lax.dot_general(leaving, x, (((1,), (1,)), ((), ())), preferred_element_type=F32).astype(BF)
    x_recv = lax.all_to_all(x_send, "front", split_axis=0, concat_axis=0, tiled=True)
    x_moved = lax.dot_general(x_recv, arriving, (((0,), (1,)), ((), ())), preferred_element_type=F32).astype(BF)
    x_new = jnp.where(staying[None, :], x, x_moved).reshape(FRAMES, SUB * mels, streams)

    keys = key_cache.transpose(1, 0, 2)
    values = value_cache.transpose(1, 0, 2)
    conv = conv_cache.transpose(1, 0, 2)
    choose = lambda a: jnp.einsum("rs,jsc->rjc", leaving, a, preferred_element_type=F32).astype(BF)
    bundle = jnp.concatenate([choose(keys), choose(values), choose(conv)], axis=1)
    recv = lax.all_to_all(bundle, "front", split_axis=0, concat_axis=0, tiled=True).transpose(1, 0, 2)
    keys_recv, values_recv = recv[:CACHE], recv[CACHE : 2 * CACHE]
    conv_moved = jnp.einsum(
        "sr,jrc->jsc", arriving, recv[2 * CACHE :], preferred_element_type=F32
    ).astype(BF)
    conv_old = jnp.where(staying[None, :, None], conv, conv_moved)

    groups = streams // GROUP
    span = max(1, 256 // slots)
    pick = jnp.einsum(
        "ab,gnr->ganbr", jnp.eye(span, dtype=BF), arriving.reshape(groups, GROUP, slots)
    ).reshape(groups, span * GROUP, span * slots)
    has = jnp.sum((~staying).astype(jnp.int32).reshape(groups, GROUP), axis=1)
    valid_wide = jnp.broadcast_to(valid_new.astype(F32)[:, None], (streams, local))
    bits = jnp.stack([(valid_new >> b) & 1 for b in range(3)]).astype(BF)
    bits = jnp.broadcast_to(bits[:, :, None], (3, streams, local))
    stay_wide = jnp.broadcast_to(staying.astype(BF)[:, None], (streams, local))
    position = jnp.arange(TOTAL, dtype=jnp.int32)[:, None]
    cache_ok = (position < CACHE) & (position >= CACHE - cache_fill[None, :])
    new_ok = (position >= CACHE) & (position - CACHE < valid_new[None, :])
    colbias = jnp.where(cache_ok | new_ok, 0.0, masked_score).astype(F32)
    colbias = colbias.reshape(TOTAL, groups, GROUP).transpose(1, 0, 2).reshape(groups, 1, TOTAL * GROUP)
    row_of = jnp.arange(FRAMES * GROUP, dtype=jnp.int32) % GROUP
    col_of = jnp.arange(TOTAL * GROUP, dtype=jnp.int32) % GROUP
    match = jnp.where(row_of[:, None] == col_of[None, :], 0.0, masked_score).astype(F32)

    inputs, queries, key_new, value_new = project(
        x_new, sub_full, bias_full, ln1_gain[None], w_query, w_key, w_value
    )
    context, key_out, value_out = attend(
        has, queries, key_new, value_new, keys, values, keys_recv, values_recv, pick, bits, stay_wide,
        colbias, match,
    )
    context_full = lax.all_gather(context, "enc")
    middle, activated, conv_out = convolve(
        context_full, inputs, attn_full, ln2_gain[None], w_glu_value, w_glu_gate, conv_old, bits,
        depth_kernel, norm_scale[None], norm_shift[None],
    )
    act_full = lax.all_gather(activated, "enc")
    encoded = finish(member.astype(jnp.int32)[None], act_full, conv_cols, middle, valid_wide)
    back = lambda a: a.transpose(1, 0, 2)
    return back(encoded), back(key_out), back(value_out), back(conv_out)


def solution(mesh):
    in_specs = (
        P("front", None, None),
        P(None, "enc"),
        P("enc"),
        P("front", None, "enc"),
        P("front", None, "enc"),
        P("front", None, "enc"),
        P("front"),
        P("front"),
        P("front"),
        P("front"),
        P(),
        P(None, "enc"),
        P(None, "enc"),
        P(None, "enc"),
        P("enc", None),
        P(),
        P(None, "enc"),
        P(None, "enc"),
        P(None, "enc"),
        P("enc"),
        P("enc"),
        P("enc", None),
    )
    out_specs = (P("front", None, "enc"),) * 4
    return jax.shard_map(
        on_device, mesh=mesh, in_specs=in_specs, out_specs=out_specs, check_vma=False
    )
```

profile of v0, /device:TPU:0, one launch (start us, length us, event | category | flops | bytes accessed | tf_op | source)
XLA Modules:
  0.0 212.7 jit_solution(14106821895828366771)
XLA Ops:
  7.2 0.0 all-gather.11.cloned.1.call-start
  7.2 0.7 all-gather.11.cloned.1.call-update
  7.9 0.7 and_select_fusion.1
  8.6 0.2 convert_reduce_fusion.1
  8.8 0.7 compare_select_fusion.1
  9.4 1.7 convolution_convert_fusion.1
  11.1 0.7 all_to_all.25
  11.8 5.2 %all-to-all-start = ((bf16[8,2,4480]{2,1,0:T(2,128)(2,1)}), bf16[8,2,4480]{2,1,0:T(2,128)(2,1)S(1)}, u32[]{:S(2)}, u32[]{:S(2)}) async-start(bf16[8,2,4480]{2,1,0:T(2,128)(2,1)} %all_to_all.25), calls=%async_computation | async-start | bytes 286720 | tf_op jit(solution)/shard_map/all_to_all | solution.py:314
  17.0 0.0 all-gather.9.cloned.1.call-start
  17.0 0.7 all-gather.9.cloned.1.call-update
  17.8 0.2 convert_reduce_fusion
  18.0 0.1 eq.101
  18.1 3.3 %convolution_convert_fusion.2 = bf16[16,70,256]{2,0,1:T(8,128)(2,1)S(1)} fusion(s32[128]{0:T(128)S(1)} %compare_select_fusion.1, bf16[128,70,256]{2,0,1:T(8,128)(2,1)} %param.26), kind=kOutput, calls=%fused_computation.4 | convolution fusion | flops 73689088 | bytes 5161472 | tf_op jit(solution)/shard_map/rs,jsc->rjc/dot_general | solution.py:321
  21.4 0.7 copy-done
  22.1 0.7 convolution_convert_fusion.3
  22.8 0.3 copy-done.3
  23.1 0.2 convolution_convert_fusion.5
  23.3 0.2 pad_maximum_fusion
  23.5 0.4 copy-done.8
  24.0 0.1 fusion.6
  24.1 3.9 %multiply_bitcast_fusion = bf16[8,16,16,16,16]{4,3,2,1,0:T(8,128)(2,1)} fusion(bf16[16,16]{1,0:T(8,128)(2,1)S(1)} %fusion.15, bf16[8,16,16]{2,1,0:T(8,128)(2,1)S(1)} %fusion.6), kind=kLoop, calls=%fused_computation | loop fusion | flops 524288 | bytes 1053184 | tf_op jit(solution)/shard_map/ab,gnr->ganbr/transpose | solution.py:332
  27.9 0.1 lt.84
  28.0 11.3 %all-gather.3 = bf16[4,1,256]{2,1,0:T(2,128)(2,1)S(1)} all-gather(bf16[1,1,256]{2,1,0:T(2,128)(2,1)S(1)} %reshape.239), channel_id=1, replica_groups=mesh['front'=8,'enc'=4] {'enc'}, dimensions={0}, use_global_device_ids=true | all-gather | bytes 2560 | tf_op jit(solution)/shard_map/all_gather | solution.py:304
  39.3 0.6 convert.25.sb_ref
  39.9 11.0 %reshape.232.pick_ref = bf16[8,256,256]{2,1,0:T(8,128)(2,1)} reshape(bf16[8,16,16,16,16]{4,3,2,1,0:T(8,128)(2,1)} %multiply_bitcast_fusion) | data formatting | bytes 2097152 | tf_op jit(solution)/shard_map/reshape | solution.py:334
  50.9 1.4 copy.45
  52.4 0.1 reshape.234
  52.4 0.1 ge.39
  52.6 0.2 ge.44
  52.8 0.2 lt.90
  53.0 0.1 lt.81
  53.0 0.1 lt.82
  53.1 0.1 ge.37
  53.2 0.1 and.99
  53.3 0.1 and.100
  53.4 0.1 and.95
  53.5 0.1 and.96
  53.6 0.7 reduce_sum.27.has_ref
  54.2 4.2 %all-to-all-start.1 = ((bf16[16,148,256]{2,1,0:T(8,128)(2,1)}), bf16[16,148,256]{2,1,0:T(8,128)(2,1)S(1)}, u32[]{:S(2)}, u32[]{:S(2)}) async-start(bf16[16,148,256]{2,1,0:T(8,128)(2,1)} %copy.45), calls=%async_computation.1 | async-start | bytes 2490368 | tf_op jit(solution)/shard_map/all_to_all | solution.py:323
  58.4 0.0 all-gather.13.cloned.1.call-start
  58.5 0.7 or_select_fusion.colbias_ref
  59.2 0.9 compare_select_fusion.match_ref
  60.1 0.1 all_to_all.27
  60.2 1.5 fusion
  61.7 14.2 %all-to-all-done.1 = bf16[16,148,256]{2,1,0:T(8,128)(2,1)S(1)} async-done(((bf16[16,148,256]{2,1,0:T(8,128)(2,1)}), bf16[16,148,256]{2,1,0:T(8,128)(2,1)S(1)}, u32[]{:S(2)}, u32[]{:S(2)}) %all-to-all-start.1) | async-done | bytes 1212448 | tf_op jit(solution)/shard_map/all_to_all | solution.py:323
  76.0 0.2 copy.61
  76.2 1.1 fusion.26
  77.3 10.0 %project.1 = (bf16[7,128,1024]{2,1,0:T(8,128)(2,1)}, bf16[7,128,256]{2,1,0:T(8,128)(2,1)}, bf16[7,128,256]{2,1,0:T(8,128)(2,1)}, bf16[7,128,256]{2,1,0:T(8,128)(2,1)}) custom-call(bf16[7,640,128]{2,1,0:T(8,128)(2,1)} %bitcast.69, bf16[4,640,256]{2,1,0:T(8,128)(2,1)} %bitcast.73, f32[1,1024]{1,0:T(1,128)} %convert.25.sb_ref, f32[1,1024]{1,0:T(1,128)} %bitcast.79, ...), custom_call_target="tpu_custom_call" | custom-call | tf_op jit(solution)/shard_map/project/pallas_call | solution.py:84
  87.3 0.8 broadcast_in_dim.101.bits_ref
  88.1 0.7 broadcast_in_dim.102.stay_ref
  88.8 17.4 %attend.1 = (bf16[7,128,256]{2,1,0:T(8,128)(2,1)}, bf16[70,128,256]{2,1,0:T(8,128)(2,1)}, bf16[70,128,256]{2,1,0:T(8,128)(2,1)}) custom-call(s32[8]{0:T(128)} %reduce_sum.27.has_ref, bf16[7,128,256]{2,1,0:T(8,128)(2,1)} %get-tuple-element.14.q_ref, bf16[7,128,256]{2,1,0:T(8,128)(2,1)} %get-tuple-element.15.kn_ref, ...), custom_call_target="tpu_custom_call" | custom-call | flops 1200000000 | bytes 20000000 | tf_op jit(solution)/shard_map/attend/pallas_call | solution.py:153
  106.2 0.0 all-gather.13.cloned.1.call-update
  106.3 0.2 all-gather.15.cloned.1.call-start
  106.5 1.2 fusion.2.conv_ref
  107.7 36.7 %all-gather.13.cloned.1.call-done = bf16[28,128,256]{2,1,0:T(8,128)(2,1)} async-done(((bf16[7,128,256]{2,1,0:T(8,128)(2,1)}), bf16[28,128,256]{2,1,0:T(8,128)(2,1)}) %all-gather.13.cloned.1.call-update) | async-done | bytes 1835024 | tf_op jit(solution)/shard_map/all_gather | solution.py:356
  144.3 9.0 %convolve.1 = (bf16[7,128,1024]{2,1,0:T(8,128)(2,1)}, bf16[7,128,256]{2,1,0:T(8,128)(2,1)}, bf16[8,128,256]{2,1,0:T(8,128)(2,1)}) custom-call(bf16[4,7,128,256]{3,2,1,0:T(8,128)(2,1)} %bitcast.72, bf16[7,128,1024]{2,1,0:T(8,128)(2,1)} %get-tuple-element.18.in_ref, bf16[1024,1024]{1,0:T(8,128)(2,1)} %all-gather.9.cloned.1.call-done.wo_ref, ...), custom_call_target="tpu_custom_call" | custom-call | tf_op jit(solution)/shard_map/convolve/pallas_call | solution.py:214
  153.3 0.0 all-gather.15.cloned.1.call-update
  153.4 0.8 copy.62
  154.2 3.5 %all-to-all-start.2 = ((bf16[256,4,256]{2,0,1:T(8,128)(2,1)}), bf16[256,4,256]{2,0,1:T(8,128)(2,1)S(1)}, u32[]{:S(2)}, u32[]{:S(2)}) async-start(bf16[256,4,256]{2,0,1:T(8,128)(2,1)} %bitcast.62), calls=%async_computation.2 | async-start | bytes 1048576 | tf_op jit(solution)/shard_map/all_to_all | solution.py:306
  157.7 1.1 copy.51
  158.8 28.1 %all-to-all-done.2 = bf16[256,4,256]{2,0,1:T(8,128)(2,1)S(1)} async-done(((bf16[256,4,256]{2,0,1:T(8,128)(2,1)}), bf16[256,4,256]{2,0,1:T(8,128)(2,1)S(1)}, u32[]{:S(2)}, u32[]{:S(2)}) %all-to-all-start.2) | async-done | bytes 524320 | tf_op jit(solution)/shard_map/all_to_all | solution.py:306
  186.8 15.6 %all-gather.15.cloned.1.call-done = bf16[28,128,256]{2,1,0:T(8,128)(2,1)} async-done(((bf16[7,128,256]{2,1,0:T(8,128)(2,1)}), bf16[28,128,256]{2,1,0:T(8,128)(2,1)}) %all-gather.15.cloned.1.call-update) | async-done | bytes 1835024 | tf_op jit(solution)/shard_map/all_gather | solution.py:361
  202.4 0.7 broadcast_in_dim.111.valid_ref
  203.2 3.0 %finish.1 = bf16[7,128,256]{2,1,0:T(8,128)(2,1)} custom-call(s32[1]{0:T(128)} %bitcast.me_ref, bf16[4,7,128,256]{3,2,1,0:T(8,128)(2,1)} %bitcast.71, bf16[1024,256]{1,0:T(8,128)(2,1)} %bitcast.70, bf16[7,128,1024]{2,1,0:T(8,128)(2,1)} %get-tuple-element.20.mid_ref, f32[128,256]{1,0:T(8,128)} %broadcast_in_dim.111.valid_ref), custom_call_target="tpu_custom_call" | custom-call | tf_op jit(solution)/shard_map/finish/pallas_call | solution.py:252
  (36 shorter events, 0.2 us)
Async XLA Ops:
  7.2 70.1 %all-gather.11.cloned.1.call-start = ((), (), s32[]{:S(2)}) async-start(), calls=%async_computation.4 | async-start | bytes 1638400 | tf_op jit(solution)/shard_map/all_gather | solution.py:303
  7.9 9.9 %copy-start.6 = (s32[128]{0:T(128)S(1)}, s32[128]{0:T(128)}, u32[]{:S(2)}) copy-start(s32[128]{0:T(128)} %param.29) | copy-start | bytes 1540
  11.8 42.4 %all-to-all-start = ((bf16[8,2,4480]{2,1,0:T(2,128)(2,1)}), bf16[8,2,4480]{2,1,0:T(2,128)(2,1)S(1)}, u32[]{:S(2)}, u32[]{:S(2)}) async-start(bf16[8,2,4480]{2,1,0:T(2,128)(2,1)} %all_to_all.25), calls=%async_computation | async-start | bytes 286720 | tf_op jit(solution)/shard_map/all_to_all | solution.py:314
  17.0 90.7 %all-gather.9.cloned.1.call-start = ((), (), s32[]{:S(2)}) async-start(), calls=%async_computation.3 | async-start | bytes 2621440 | tf_op jit(solution)/shard_map/all_gather | solution.py:305
  18.1 4.0 %copy-start = (bf16[128,70,256]{2,0,1:T(8,128)(2,1)S(1)}, bf16[128,70,256]{2,0,1:T(8,128)(2,1)}, u32[]{:S(2)}) copy-start(bf16[128,70,256]{2,0,1:T(8,128)(2,1)} %param.25) | copy-start | bytes 13762564
  22.1 1.0 copy-start.3
  22.1 1.2 copy-start.7
  23.3 0.7 copy-start.8
  24.1 4.0 %copy-start.9 = (bf16[256]{0:T(256)(128)(2,1)S(1)}, bf16[256]{0:T(256)(128)(2,1)}, u32[]{:S(2)}) copy-start(bf16[256]{0:T(256)(128)(2,1)} %param.24) | copy-start | bytes 1540
  54.2 5.9 %copy-start.1 = (bf16[128,56,80]{0,2,1:T(8,128)(2,1)S(1)}, bf16[128,56,80]{0,2,1:T(8,128)(2,1)}, u32[]{:S(2)}) copy-start(bf16[128,56,80]{0,2,1:T(8,128)(2,1)} %param.22) | copy-start | bytes 3440644
  54.2 21.7 %all-to-all-start.1 = ((bf16[16,148,256]{2,1,0:T(8,128)(2,1)}), bf16[16,148,256]{2,1,0:T(8,128)(2,1)S(1)}, u32[]{:S(2)}, u32[]{:S(2)}) async-start(bf16[16,148,256]{2,1,0:T(8,128)(2,1)} %copy.45), calls=%async_computation.1 | async-start | bytes 2490368 | tf_op jit(solution)/shard_map/all_to_all | solution.py:323
  58.4 85.9 %all-gather.13.cloned.1.call-start = ((), (), s32[]{:S(2)}) async-start(), calls=%async_computation.5 | async-start | bytes 2293760 | tf_op jit(solution)/shard_map/all_gather | solution.py:356
  106.3 96.2 %all-gather.15.cloned.1.call-start = ((), (), s32[]{:S(2)}) async-start(), calls=%async_computation.6 | async-start | bytes 2293760 | tf_op jit(solution)/shard_map/all_gather | solution.py:361
  144.3 9.1 %copy-start.4 = (bf16[256,1024]{1,0:T(8,128)(2,1)S(1)}, bf16[256,1024]{1,0:T(8,128)(2,1)}, u32[]{:S(2)}) copy-start(bf16[256,1024]{1,0:T(8,128)(2,1)} %param.43) | copy-start | bytes 1572868
  153.3 4.3 %copy-start.5 = (bf16[8,128,256]{2,1,0:T(8,128)(2,1)S(1)}, bf16[8,128,256]{2,1,0:T(8,128)(2,1)}, u32[]{:S(2)}) copy-start(bf16[8,128,256]{2,1,0:T(8,128)(2,1)} %get-tuple-element.23) | copy-start | bytes 1572868
  154.2 32.7 %all-to-all-start.2 = ((bf16[256,4,256]{2,0,1:T(8,128)(2,1)}), bf16[256,4,256]{2,0,1:T(8,128)(2,1)S(1)}, u32[]{:S(2)}, u32[]{:S(2)}) async-start(bf16[256,4,256]{2,0,1:T(8,128)(2,1)} %bitcast.62), calls=%async_computation.2 | async-start | bytes 1048576 | tf_op jit(solution)/shard_map/all_to_all | solution.py:306
  186.8 16.3 %copy-start.2 = (bf16[256,4,256]{2,0,1:T(8,128)(2,1)}, bf16[256,4,256]{2,0,1:T(8,128)(2,1)S(1)}, u32[]{:S(2)}) copy-start(bf16[256,4,256]{2,0,1:T(8,128)(2,1)S(1)} %all-to-all-done.2) | copy-start | bytes 1572868
Sparse Core Ops, SparseCore 0:
  9.6 35.4 all-gather.10
  46.6 44.9 all-gather.8
  106.4 37.8 all-gather.12
  153.5 48.9 all-gather.14
where the time goes:
time: 214 us; the launch traced here: 213 us
  waiting for transfers between devices  96 us (45%)
  Pallas kernels  39.5 us (18%)
  local copies, waits for them, and re-layouts  21.5 us (10%)
  between operations  14 us (7%)
  starting transfers between devices  13.2 us (6%)
  blocking collectives  11.3 us (5%)
  other arithmetic  8.77 us (4%)
  matrix products  8.58 us (4%)
    all_gather x1, waiting for transfers between devices, on_device(): context_full = lax.all_gather(context, 'enc')  36.7 us
    all_to_all x1, waiting for transfers between devices, on_device(): lax.all_to_all(w_conv_out, 'enc', split_axis=1, concat_axis=0, tiled=True)  28.1 us
    pallas_call x1, Pallas kernels, attend(): pl.pallas_call(attend_kernel, grid_spec=pltpu.PrefetchScalarGridSpec(num_...  17.4 us
    all_gather x1, waiting for transfers between devices, on_device(): act_full = lax.all_gather(activated, 'enc')  15.6 us
    all_to_all x1, waiting for transfers between devices, on_device(): lax.all_to_all(bundle, 'front', split_axis=0, concat_axis=0, tiled=True)  14.2 us
    all_gather x1, blocking collectives, on_device(): bias_full = lax.all_gather(sub_bias, 'enc', tiled=True).astype(F32)[None]  11.3 us
    reshape x1, local copies, waits for them, and re-layouts, on_device(): pick = jnp.einsum('ab,gnr->ganbr', jnp.eye(span, dtype=BF), arriving.resh...  11 us
    pallas_call x1, Pallas kernels, project(): pl.pallas_call(project_kernel, grid=(frames,), in_specs=[pl.BlockSpec((1,...  10 us
  transfers between devices with their start and end apart: 7, of which 4 were waited for; matrix products, arithmetic and copies ran while one was open for 17% of the time, Pallas kernels for 13%

commit v1 on v0

--- a/solution.py
+++ b/solution.py
@@ -61,13 +61,14 @@
     return block
 
 
-def project_kernel(x_ref, sw_ref, sb_ref, gain_ref, wq_ref, wk_ref, wv_ref, in_ref, q_ref, k_ref, v_ref):
+def project_kernel(x_ref, sw_ref, gain_ref, wq_ref, wk_ref, wv_ref, in_ref, q_ref, k_ref, v_ref):
     x = x_ref[0]
+    depth = x.shape[0]
     parts = []
     for g in range(sw_ref.shape[0]):
-        part = lax.dot_general(x, sw_ref[g], (((0,), (0,)), ((), ())), preferred_element_type=F32)
-        parts.append(part)
-    inputs = (jnp.concatenate(parts, axis=1) + sb_ref[...]).astype(BF)
+        part = lax.dot_general(x, sw_ref[g, :depth], (((0,), (0,)), ((), ())), preferred_element_type=F32)
+        parts.append(part + sw_ref[g, depth : depth + 1, :].astype(F32))
+    inputs = jnp.concatenate(parts, axis=1).astype(BF)
     in_ref[0] = inputs
     normed = layer_norm(inputs.astype(F32), gain_ref[...]).astype(BF)
     q_ref[0] = mm(normed, wq_ref[...]).astype(BF)
@@ -75,7 +76,7 @@
     v_ref[0] = mm(normed, wv_ref[...]).astype(BF)
 
 
-def project(x, sw, sb, gain, wq, wk, wv):
+def project(x, sw, gain, wq, wk, wv):
     frames, depth, streams = x.shape
     width = wq.shape[0]
     local = wq.shape[1]
@@ -87,7 +88,6 @@
         in_specs=[
             pl.BlockSpec((1, depth, streams), lambda t: (t, 0, 0)),
             whole(sw.shape),
-            whole(sb.shape),
             whole(gain.shape),
             whole(wq.shape),
             whole(wk.shape),
@@ -98,7 +98,7 @@
         + [jax.ShapeDtypeStruct((frames, streams, local), BF)] * 3,
         compiler_params=pltpu.CompilerParams(vmem_limit_bytes=VMEM_LIMIT),
         name="project",
-    )(x, sw, sb, gain, wq, wk, wv)
+    )(x, sw, gain, wq, wk, wv)
 
 
 def attend_kernel(
@@ -136,7 +136,7 @@
         peak = jnp.max(scores, axis=-1, keepdims=True)
         expo = jnp.exp(scores - peak)
         weights = (expo * (1.0 / jnp.sum(expo, axis=-1, keepdims=True))).astype(BF)
-        ctx_ref[:, :, lanes] = mm(weights, vh).astype(BF).reshape(FRAMES, GROUP, HEAD)
+        ctx_ref[0, :, lanes] = mm(weights, vh).astype(BF)
     masks = [bits_ref[b] > 0.5 for b in range(3)]
     step = 10
     for src, dst in ((kall, ko_ref), (vall, vo_ref)):
@@ -164,11 +164,13 @@
                 pl.BlockSpec((1, 1, TOTAL * GROUP), lambda g, *_: (g, 0, 0)),
                 whole(match.shape),
             ],
-            out_specs=[block(FRAMES), block(CACHE), block(CACHE)],
+            out_specs=[
+                pl.BlockSpec((1, FRAMES * GROUP, local), lambda g, *_: (g, 0, 0)), block(CACHE), block(CACHE),
+            ],
             scratch_shapes=[pltpu.VMEM((TOTAL, GROUP, local), BF)] * 2,
         ),
         out_shape=[
-            jax.ShapeDtypeStruct((FRAMES, streams, local), BF),
+            jax.ShapeDtypeStruct((groups, FRAMES * GROUP, local), BF),
             jax.ShapeDtypeStruct((CACHE, streams, local), BF),
             jax.ShapeDtypeStruct((CACHE, streams, local), BF),
         ],
@@ -178,94 +180,192 @@
     )(has, q, kn, vn, kc, vc, kr, vr, pick, bits, stay, colbias, match)
 
 
-def convolve_kernel(
-    ctx_ref, in_ref, wo_ref, gain_ref, wv_ref, wg_ref, conv_ref, bits_ref, dk_ref, scale_ref, bias_ref,
-    mid_ref, act_ref, co_ref, conv_all,
+def tail_kernel(
+    parts, chunks, ctx_ref, in_ref, wo_ref, gain_ref, wv_ref, wg_ref, conv_ref, bits_ref, dk_ref, scale_ref,
+    bias_ref, wc_ref, valid_ref, enc_ref, co_ref, ctx_all, act_all, middle_own, middle_now, conv_all,
+    ctx_send, ctx_recv, act_send, act_recv,
 ):
-    parts, frames, streams, local = ctx_ref.shape
+    me = lax.axis_index("enc")
+    local = ctx_ref.shape[2]
     width = in_ref.shape[2]
-    rows = frames * streams
-    attended = jnp.zeros((rows, width), F32)
-    for g in range(parts):
-        share = mm(ctx_ref[g].reshape(rows, local), wo_ref[g * local : (g + 1) * local])
-        attended = attended + share.astype(BF).astype(F32)
-    middle = (in_ref[...].reshape(rows, width).astype(F32) + attended).astype(BF)
-    mid_ref[...] = middle.reshape(frames, streams, width)
-    normed = layer_norm(middle.astype(F32), gain_ref[...]).astype(BF)
-    gated = (mm(normed, wv_ref[...]) * jax.nn.sigmoid(mm(normed, wg_ref[...]))).astype(BF)
-    conv_all[0:CONV_CACHE] = conv_ref[...]
-    conv_all[CONV_CACHE:] = gated.reshape(frames, streams, local)
-    taps = [dk_ref[k : k + 1, :] for k in range(KERNEL)]
-    for t in range(frames):
-        total = jnp.zeros((streams, local), F32)
-        for k in range(KERNEL):
-            total = total + taps[k] * conv_all[t + k].astype(F32)
-        shaped = total * scale_ref[...] + bias_ref[...]
-        act_ref[t] = (shaped * jax.nn.sigmoid(shaped)).astype(BF)
-    co_ref[...] = shift_rows(conv_all[...], [bits_ref[b] > 0.5 for b in range(3)])
-
-
-def convolve(ctx, inputs, wo, gain, wv, wg, conv, bits, dk, scale, bias):
-    parts, frames, streams, local = ctx.shape
-    width = inputs.shape[2]
-    size = min(64, streams)
-    whole = lambda shape: pl.BlockSpec(shape, lambda g: (0,) * len(shape))
-    block = lambda n, w: pl.BlockSpec((n, size, w), lambda g: (0, g, 0))
+    rows = FRAMES * GROUP
+    last = parts - 1
+    right = lax.rem(me + 1, parts)
+    left = lax.rem(me + parts - 1, parts)
+    mesh_ids = pl.DeviceIdType.MESH
+
+    barrier = pltpu.get_barrier_semaphore()
+
+    @pl.when(me > 0)
+    def _():
+        pl.semaphore_signal(barrier, inc=1, device_id={"enc": left}, device_id_type=mesh_ids)
+
+    @pl.when(me < last)
+    def _():
+        pl.semaphore_signal(barrier, inc=1, device_id={"enc": right}, device_id_type=mesh_ids)
+
+    inner = (me > 0) & (me < last)
+
+    @pl.when(inner)
+    def _():
+        pl.semaphore_wait(barrier, 2)
+
+    @pl.when(jnp.logical_not(inner))
+    def _():
+        pl.semaphore_wait(barrier, 1)
+
+    def hop(line, source, chunk, way):
+        buffer, send, recv = line
+        return pltpu.make_async_remote_copy(
+            src_ref=buffer.at[source, chunk],
+            dst_ref=buffer.at[source, chunk],
+            send_sem=send.at[way, source, chunk],
+            recv_sem=recv.at[source, chunk],
+            device_id={"enc": (right, left)[way]},
+            device_id_type=mesh_ids,
+        )
+
+    def send_own(line, chunk):
+        @pl.when(me < last)
+        def _():
+            hop(line, me, chunk, 0).start()
+
+        @pl.when(me > 0)
+        def _():
+            hop(line, me, chunk, 1).start()
+
+    def pass_on(line, chunk, distance):
+        @pl.when(me >= distance)
+        def _():
+            copy = hop(line, me - distance, chunk, 0)
+            copy.wait_recv()
+
+            @pl.when(me < last)
+            def _():
+                copy.start()
+
+        @pl.when(me + distance <= last)
+        def _():
+            copy = hop(line, me + distance, chunk, 1)
+            copy.wait_recv()
+
+            @pl.when(me > 0)
+            def _():
+                copy.start()
+
+    def sent(line, chunk):
+        for source in range(parts):
+            @pl.when((me >= source) & (me < last))
+            def _():
+                hop(line, source, chunk, 0).wait_send()
+
+            @pl.when((me <= source) & (me > 0))
+            def _():
+                hop(line, source, chunk, 1).wait_send()
+
+    def convolve(chunk):
+        here = pl.ds(pl.multiple_of(chunk * GROUP, GROUP), GROUP)
+        attended = jnp.zeros((rows, width), F32)
+        for g in range(parts):
+            share = mm(ctx_all[g, chunk], wo_ref[g * local : (g + 1) * local])
+            attended = attended + share.astype(BF).astype(F32)
+        middle = (in_ref[:, here, :].reshape(rows, width).astype(F32) + attended).astype(BF)
+        middle_now[...] = middle
+        middle_own[chunk] = middle_now[:, pl.ds(pl.multiple_of(me * local, local), local)]
+        normed = layer_norm(middle.astype(F32), gain_ref[...]).astype(BF)
+        gated = (mm(normed, wv_ref[...]) * jax.nn.sigmoid(mm(normed, wg_ref[...]))).astype(BF)
+        conv_all[0:CONV_CACHE] = conv_ref[:, here, :]
+        conv_all[CONV_CACHE:] = gated.reshape(FRAMES, GROUP, local)
+        for t in range(FRAMES):
+            total = jnp.zeros((GROUP, local), F32)
+            for k in range(KERNEL):
+                total = total + dk_ref[k : k + 1, :] * conv_all[t + k].astype(F32)
+            shaped = total * scale_ref[...] + bias_ref[...]
+            active = (shaped * jax.nn.sigmoid(shaped)).astype(BF)
+            act_all[me, chunk, t * GROUP : (t + 1) * GROUP] = active
+        masks = [bits_ref[b, here, :] > 0.5 for b in range(3)]
+        co_ref[:, here, :] = shift_rows(conv_all[...], masks)
+
+    def finish(chunk):
+        here = pl.ds(pl.multiple_of(chunk * GROUP, GROUP), GROUP)
+        total = jnp.zeros((rows, local), F32)
+        for g in range(parts):
+            share = mm(act_all[g, chunk], wc_ref[g * local : (g + 1) * local])
+            total = total + share.astype(BF).astype(F32)
+        total = (total + middle_own[chunk].astype(F32)).reshape(FRAMES, GROUP, local)
+        valid = valid_ref[here, :]
+        for t in range(FRAMES):
+            enc_ref[t, here, :] = jnp.where(valid > t + 0.5, total[t], 0.0).astype(BF)
+
+    ctx_all[me] = ctx_ref[...]
+    ctx_line = (ctx_all, ctx_send, ctx_recv)
+    act_line = (act_all, act_send, act_recv)
+
+    def turn(step, carry):
+        def at(lag, action):
+            chunk = step - lag
+
+            @pl.when((chunk >= 0) & (chunk < chunks))
+            def _():
+                action(chunk)
+
+        def middle_part(chunk):
+            pass_on(ctx_line, chunk, last)
+            convolve(chunk)
+            send_own(act_line, chunk)
+
+        def end_part(chunk):
+            pass_on(act_line, chunk, last)
+            finish(chunk)
+
+        at(0, lambda c: send_own(ctx_line, c))
+        for d in range(1, last):
+            at(d, lambda c, d=d: pass_on(ctx_line, c, d))
+        at(last, middle_part)
+        for d in range(1, last):
+            at(last + d, lambda c, d=d: pass_on(act_line, c, d))
+        at(2 * last, end_part)
+        return carry
+
+    lax.fori_loop(0, chunks + 2 * last, turn, 0)
+
+    def drain(chunk, carry):
+        sent(ctx_line, chunk)
+        sent(act_line, chunk)
+        return carry
+
+    lax.fori_loop(0, chunks, drain, 0)
+
+
+def tail(parts, ctx, inputs, wo, gain, wv, wg, conv, bits, dk, scale, bias, wc, valid_wide):
+    chunks, rows, local = ctx.shape
+    frames, streams, width = inputs.shape
+    vmem = pl.BlockSpec(memory_space=pltpu.VMEM)
     return pl.pallas_call(
-        convolve_kernel,
-        grid=(streams // size,),
-        in_specs=[
-            pl.BlockSpec((parts, frames, size, local), lambda g: (0, 0, g, 0)),
-            block(frames, width),
-            whole(wo.shape), whole(gain.shape), whole(wv.shape), whole(wg.shape),
-            block(CONV_CACHE, local), block(3, local),
-            whole(dk.shape), whole(scale.shape), whole(bias.shape),
-        ],
-        out_specs=[block(frames, width), block(frames, local), block(CONV_CACHE, local)],
+        functools.partial(tail_kernel, parts, chunks),
+        in_specs=[vmem] * 13,
+        out_specs=[vmem] * 2,
         out_shape=[
-            jax.ShapeDtypeStruct((frames, streams, width), BF),
             jax.ShapeDtypeStruct((frames, streams, local), BF),
             jax.ShapeDtypeStruct((CONV_CACHE, streams, local), BF),
         ],
-        scratch_shapes=[pltpu.VMEM((CONV_CACHE + frames, size, local), BF)],
-        compiler_params=pltpu.CompilerParams(vmem_limit_bytes=VMEM_LIMIT),
-        name="convolve",
-    )(ctx, inputs, wo, gain, wv, wg, conv, bits, dk, scale, bias)
-
-
-def finish_kernel(me_ref, act_ref, wc_ref, mid_ref, valid_ref, out_ref):
-    parts, frames, streams, local = act_ref.shape
-    rows = frames * streams
-    total = jnp.zeros((rows, local), F32)
-    for g in range(parts):
-        share = mm(act_ref[g].reshape(rows, local), wc_ref[g * local : (g + 1) * local])
-        total = total + share.astype(BF).astype(F32)
-    total = total + mid_ref[...].reshape(rows, local).astype(F32)
-    total = total.reshape(frames, streams, local)
-    for t in range(frames):
-        out_ref[t] = jnp.where(valid_ref[...] > t + 0.5, total[t], 0.0).astype(BF)
-
-
-def finish(me, act, wc, middle, valid_wide):
-    parts, frames, streams, local = act.shape
-    size = min(64, streams)
-    return pl.pallas_call(
-        finish_kernel,
-        grid_spec=pltpu.PrefetchScalarGridSpec(
-            num_scalar_prefetch=1,
-            grid=(streams // size,),
-            in_specs=[
-                pl.BlockSpec((parts, frames, size, local), lambda g, m: (0, 0, g, 0)),
-                pl.BlockSpec(wc.shape, lambda g, m: (0, 0)),
-                pl.BlockSpec((frames, size, local), lambda g, m: (0, g, m[0])),
-                pl.BlockSpec((size, local), lambda g, m: (g, 0)),
-            ],
-            out_specs=pl.BlockSpec((frames, size, local), lambda g, m: (0, g, 0)),
+        scratch_shapes=[
+            pltpu.VMEM((parts, chunks, rows, local), BF),
+            pltpu.VMEM((parts, chunks, rows, local), BF),
+            pltpu.VMEM((chunks, rows, local), BF),
+            pltpu.VMEM((rows, width), BF),
+            pltpu.VMEM((CONV_CACHE + frames, GROUP, local), BF),
+            pltpu.SemaphoreType.DMA((2, parts, chunks)),
+            pltpu.SemaphoreType.DMA((parts, chunks)),
+            pltpu.SemaphoreType.DMA((2, parts, chunks)),
+            pltpu.SemaphoreType.DMA((parts, chunks)),
+        ],
+        compiler_params=pltpu.CompilerParams(
+            vmem_limit_bytes=VMEM_LIMIT, collective_id=0, has_side_effects=True
         ),
-        out_shape=jax.ShapeDtypeStruct((frames, streams, local), BF),
-        compiler_params=pltpu.CompilerParams(vmem_limit_bytes=VMEM_LIMIT),
-        name="finish",
-    )(me, act, wc, middle, valid_wide)
+        cost_estimate=pl.CostEstimate(flops=4000000000, bytes_accessed=10000000, transcendentals=1000000),
+        name="tail",
+    )(ctx, inputs, wo, gain, wv, wg, conv, bits, dk, scale, bias, wc, valid_wide)
 
 
 def on_device(
@@ -294,14 +394,13 @@
 ):
     peer_count = lax.axis_size("front")
     own_index = lax.axis_index("front")
-    member = lax.axis_index("enc")
     streams = spectra.shape[0]
     local = w_query.shape[1]
     slots = peer_count * CAP
     mels = spectra.shape[2]
 
-    sub_full = lax.all_gather(sub_weight, "enc")
-    bias_full = lax.all_gather(sub_bias, "enc", tiled=True).astype(F32)[None]
+    bias_rows = jnp.broadcast_to(sub_bias[None], (16, local))
+    sub_full = lax.all_gather(jnp.concatenate([sub_weight, bias_rows], axis=0), "enc")
     attn_full = lax.all_gather(w_attn_out, "enc", tiled=True)
     conv_cols = lax.all_to_all(w_conv_out, "enc", split_axis=1, concat_axis=0, tiled=True)
 
@@ -320,6 +419,7 @@
     conv = conv_cache.transpose(1, 0, 2)
     choose = lambda a: jnp.einsum("rs,jsc->rjc", leaving, a, preferred_element_type=F32).astype(BF)
     bundle = jnp.concatenate([choose(keys), choose(values), choose(conv)], axis=1)
+    bundle, conv_cols = lax.optimization_barrier((bundle, conv_cols))
     recv = lax.all_to_all(bundle, "front", split_axis=0, concat_axis=0, tiled=True).transpose(1, 0, 2)
     keys_recv, values_recv = recv[:CACHE], recv[CACHE : 2 * CACHE]
     conv_moved = jnp.einsum(
@@ -329,9 +429,13 @@
 
     groups = streams // GROUP
     span = max(1, 256 // slots)
-    pick = jnp.einsum(
-        "ab,gnr->ganbr", jnp.eye(span, dtype=BF), arriving.reshape(groups, GROUP, slots)
-    ).reshape(groups, span * GROUP, span * slots)
+    wanted = jnp.tile(arrival.reshape(groups, GROUP), (1, span))
+    spot = jnp.arange(span * slots, dtype=jnp.int32)
+    block_of = jnp.arange(span * GROUP, dtype=jnp.int32) // GROUP
+    pick = (
+        (wanted[:, :, None] == (spot % slots)[None, None, :])
+        & (block_of[:, None] == (spot // slots)[None, :])[None]
+    ).astype(BF)
     has = jnp.sum((~staying).astype(jnp.int32).reshape(groups, GROUP), axis=1)
     valid_wide = jnp.broadcast_to(valid_new.astype(F32)[:, None], (streams, local))
     bits = jnp.stack([(valid_new >> b) & 1 for b in range(3)]).astype(BF)
@@ -347,19 +451,16 @@
     match = jnp.where(row_of[:, None] == col_of[None, :], 0.0, masked_score).astype(F32)
 
     inputs, queries, key_new, value_new = project(
-        x_new, sub_full, bias_full, ln1_gain[None], w_query, w_key, w_value
+        x_new, sub_full, ln1_gain[None], w_query, w_key, w_value
     )
     context, key_out, value_out = attend(
         has, queries, key_new, value_new, keys, values, keys_recv, values_recv, pick, bits, stay_wide,
         colbias, match,
     )
-    context_full = lax.all_gather(context, "enc")
-    middle, activated, conv_out = convolve(
-        context_full, inputs, attn_full, ln2_gain[None], w_glu_value, w_glu_gate, conv_old, bits,
-        depth_kernel, norm_scale[None], norm_shift[None],
+    encoded, conv_out = tail(
+        lax.axis_size("enc"), context, inputs, attn_full, ln2_gain[None], w_glu_value, w_glu_gate, conv_old,
+        bits, depth_kernel, norm_scale[None], norm_shift[None], conv_cols, valid_wide,
     )
-    act_full = lax.all_gather(activated, "enc")
-    encoded = finish(member.astype(jnp.int32)[None], act_full, conv_cols, middle, valid_wide)
     back = lambda a: a.transpose(1, 0, 2)
     return back(encoded), back(key_out), back(value_out), back(conv_out)
 

time: 214 us -> 187 us (0.87)
  waiting for transfers between devices: 96 us -> 25.6 us
  Pallas kernels: 39.5 us -> 96.7 us
  blocking collectives: 11.3 us -> 0 us
  local copies, waits for them, and re-layouts: 21.5 us -> 15.7 us
  other arithmetic: 8.77 us -> 12 us
    pallas_call x2 -> x1, Pallas kernels: 12 us -> 68.9 us  [tail(): pl.pallas_call(functools.partial(tail_kernel, parts, chunks), in_specs=[v...]
    all_gather x3 -> x1, waiting for transfers between devices: 52.3 us -> 0.01 us  [on_device(): lax.all_gather(jnp.concatenate([sub_weight, bias_rows], axis=0), 'enc')]
    all_to_all x1, waiting for transfers between devices: 28.1 us -> 8.62 us  [on_device(): lax.all_to_all(w_conv_out, 'enc', split_axis=1, concat_axis=0, tiled=True)]
    all_gather x1 -> x0, blocking collectives: 11.3 us -> none  [on_device(): bias_full = lax.all_gather(sub_bias, 'enc', tiled=True).astype(F32)[None]]
    reshape x1 -> x0, local copies, waits for them, and re-layouts: 11 us -> none  [on_device(): pick = jnp.einsum('ab,gnr->ganbr', jnp.eye(span, dtype=BF), arriving.resh...]
    transpose x1 -> x0, other arithmetic: 3.87 us -> none  [on_device(): jnp.einsum('ab,gnr->ganbr', jnp.eye(span, dtype=BF), arriving.reshape(gro...]
    all_to_all x1, waiting for transfers between devices: 0.01 us -> 3.54 us  [on_device(): lax.all_to_all(x_send, 'front', split_axis=0, concat_axis=0, tiled=True)]
    all_to_all x1, starting transfers between devices: 3.47 us -> 6.32 us  [on_device(): lax.all_to_all(w_conv_out, 'enc', split_axis=1, concat_axis=0, tiled=True)]
  transfers between devices with their start and end apart: 7 -> 5, of which waited for: 4 -> 3; matrix products, arithmetic and copies ran while one was open for 17% -> 15% of each run, Pallas kernels for 13% -> 15%
where the time goes in v1:
time: 187 us; the launch traced here: 186 us
  Pallas kernels  96.7 us (52%)
  waiting for transfers between devices  25.6 us (14%)
  local copies, waits for them, and re-layouts  15.7 us (8%)
  between operations  14.4 us (8%)
  starting transfers between devices  13.7 us (7%)
  other arithmetic  12 us (6%)
  matrix products  7.9 us (4%)
    pallas_call x1, Pallas kernels, tail(): pl.pallas_call(functools.partial(tail_kernel, parts, chunks), in_specs=[v...  68.9 us
    pallas_call x1, Pallas kernels, attend(): pl.pallas_call(attend_kernel, grid_spec=pltpu.PrefetchScalarGridSpec(num_...  17.7 us
    all_to_all x1, waiting for transfers between devices, on_device(): lax.all_to_all(bundle, 'front', split_axis=0, concat_axis=0, tiled=True)  12.7 us
    pallas_call x1, Pallas kernels, project(): pl.pallas_call(project_kernel, grid=(frames,), in_specs=[pl.BlockSpec((1,...  10 us
    all_to_all x1, waiting for transfers between devices, on_device(): lax.all_to_all(w_conv_out, 'enc', split_axis=1, concat_axis=0, tiled=True)  8.62 us
    all_to_all x1, starting transfers between devices, on_device(): lax.all_to_all(w_conv_out, 'enc', split_axis=1, concat_axis=0, tiled=True)  6.32 us
    dot_general x3, matrix products, on_device(): jnp.einsum('rs,jsc->rjc', leaving, a, preferred_element_type=F32).astype(BF)  4.79 us
    unnamed x60, local copies, waits for them, and re-layouts  4.59 us
  transfers between devices with their start and end apart: 5, of which 3 were waited for; matrix products, arithmetic and copies ran while one was open for 15% of the time, Pallas kernels for 15%

profile of v1, /device:TPU:0, one launch (start us, length us, event | category | flops | bytes accessed | tf_op | source)
XLA Modules:
  0.0 185.9 jit_solution(16348420624064148118)
XLA Ops:
  7.2 0.0 all-gather.6.cloned.1.call-start
  7.2 0.7 broadcast_in_dim.52
  7.9 1.7 pad_maximum_fusion.1
  9.6 0.0 all-gather.6.cloned.1.call-update
  9.7 0.8 copy.62
  10.5 6.3 %all-to-all-start.1 = ((bf16[256,4,256]{2,0,1:T(8,128)(2,1)}), bf16[256,4,256]{2,0,1:T(8,128)(2,1)}, u32[]{:S(2)}, u32[]{:S(2)}) async-start(bf16[256,4,256]{2,0,1:T(8,128)(2,1)} %bitcast.53), calls=%async_computation.1 | async-start | bytes 1048576 | tf_op jit(solution)/shard_map/all_to_all | solution.py:405
  16.9 0.7 all-gather.4.cloned.1.call-update
  17.6 0.6 and_select_fusion.1
  18.2 0.5 fusion.24
  18.7 0.8 convert_reduce_fusion
  19.5 0.2 convert_reduce_fusion.1
  19.7 0.4 convolution_convert_fusion.1
  20.1 3.3 %convolution_convert_fusion.2 = bf16[16,70,256]{2,0,1:T(8,128)(2,1)S(1)} fusion(s32[128]{0:T(128)S(1)} %compare_select_fusion.1, bf16[128,70,256]{2,0,1:T(8,128)(2,1)} %param.26), kind=kOutput, calls=%fused_computation.4 | convolution fusion | flops 73689088 | bytes 5161472 | tf_op jit(solution)/shard_map/rs,jsc->rjc/dot_general | solution.py:420
  23.4 0.5 copy-done
  24.0 0.7 convolution_convert_fusion.3
  24.7 0.3 copy-done.5
  25.0 0.8 convolution_convert_fusion.5
  25.8 0.6 fusion.26
  26.4 0.5 not_convert_fusion
  26.9 0.1 lt.91
  27.0 0.7 all_to_all.25
  27.7 0.1 ge.39
  27.8 0.2 ge.44
  28.0 0.8 lt.97
  28.8 0.1 lt.88
  28.9 0.1 lt.89
  29.0 0.7 ge.37
  29.7 0.1 and.140
  29.8 0.6 and.141
  30.4 0.1 and.144
  30.5 0.7 and.145
  31.2 1.0 pad_maximum_fusion
  32.3 0.6 add_select_fusion.1
  32.9 0.5 and_select_fusion.2
  33.4 0.7 broadcast_compare_fusion
  34.1 0.7 or_select_fusion.colbias_ref
  34.8 8.6 %all-to-all-done.1 = bf16[256,4,256]{2,0,1:T(8,128)(2,1)} async-done(((bf16[256,4,256]{2,0,1:T(8,128)(2,1)}), bf16[256,4,256]{2,0,1:T(8,128)(2,1)}, u32[]{:S(2)}, u32[]{:S(2)}) %all-to-all-start.1) | async-done | bytes 524320 | tf_op jit(solution)/shard_map/all_to_all | solution.py:405
  43.5 3.8 %all-to-all-start = ((bf16[8,2,4480]{2,1,0:T(2,128)(2,1)}), bf16[8,2,4480]{2,1,0:T(2,128)(2,1)S(1)}, u32[]{:S(2)}, u32[]{:S(2)}) async-start(bf16[8,2,4480]{2,1,0:T(2,128)(2,1)} %all_to_all.25), calls=%async_computation | async-start | bytes 286720 | tf_op jit(solution)/shard_map/all_to_all | solution.py:413
  47.2 0.7 pad_maximum_fusion.2
  47.9 1.4 copy.46
  49.3 3.5 %all-to-all-done = bf16[8,2,4480]{2,1,0:T(2,128)(2,1)S(1)} async-done(((bf16[8,2,4480]{2,1,0:T(2,128)(2,1)}), bf16[8,2,4480]{2,1,0:T(2,128)(2,1)S(1)}, u32[]{:S(2)}, u32[]{:S(2)}) %all-to-all-start) | async-done | bytes 143392 | tf_op jit(solution)/shard_map/all_to_all | solution.py:413
  52.9 0.7 copy-done.2
  53.5 3.6 %all-to-all-start.2 = ((bf16[16,148,256]{2,1,0:T(8,128)(2,1)}), bf16[16,148,256]{2,1,0:T(8,128)(2,1)S(1)}, u32[]{:S(2)}, u32[]{:S(2)}) async-start(bf16[16,148,256]{2,1,0:T(8,128)(2,1)} %copy.46), calls=%async_computation.2 | async-start | bytes 2490368 | tf_op jit(solution)/shard_map/all_to_all | solution.py:423
  57.2 0.1 tile.9
  57.2 0.1 tile.11
  57.3 0.1 reshape.291
  57.4 0.6 reduce_sum.27.has_ref
  58.1 1.3 and_convert_fusion.pick_ref
  59.3 0.9 compare_select_fusion.match_ref
  60.3 0.1 all_to_all.27
  60.3 1.5 fusion
  61.9 12.7 %all-to-all-done.2 = bf16[16,148,256]{2,1,0:T(8,128)(2,1)S(1)} async-done(((bf16[16,148,256]{2,1,0:T(8,128)(2,1)}), bf16[16,148,256]{2,1,0:T(8,128)(2,1)S(1)}, u32[]{:S(2)}, u32[]{:S(2)}) %all-to-all-start.2) | async-done | bytes 1212448 | tf_op jit(solution)/shard_map/all_to_all | solution.py:423
  74.6 0.2 copy.61
  74.8 1.2 fusion.2.conv_ref
  76.0 1.2 fusion.25
  77.1 10.0 %project.1 = (bf16[7,128,1024]{2,1,0:T(8,128)(2,1)}, bf16[7,128,256]{2,1,0:T(8,128)(2,1)}, bf16[7,128,256]{2,1,0:T(8,128)(2,1)}, bf16[7,128,256]{2,1,0:T(8,128)(2,1)}) custom-call(bf16[7,640,128]{2,1,0:T(8,128)(2,1)} %bitcast.58, bf16[4,656,256]{2,1,0:T(8,128)(2,1)} %bitcast.61, f32[1,1024]{1,0:T(1,128)} %bitcast.65, bf16[1024,256]{1,0:T(8,128)(2,1)} %wq_ref.1, ...), custom_call_target="tpu_custom_call" | custom-call | tf_op jit(solution)/shard_map/project/pallas_call | solution.py:85
  87.2 0.8 broadcast_in_dim.54.bits_ref
  88.0 0.7 broadcast_in_dim.57.stay_ref
  88.7 17.7 %attend.1 = (bf16[8,112,256]{2,1,0:T(8,128)(2,1)}, bf16[70,128,256]{2,1,0:T(8,128)(2,1)}, bf16[70,128,256]{2,1,0:T(8,128)(2,1)}) custom-call(s32[8]{0:T(128)} %reduce_sum.27.has_ref, bf16[7,128,256]{2,1,0:T(8,128)(2,1)} %get-tuple-element.15.q_ref, bf16[7,128,256]{2,1,0:T(8,128)(2,1)} %get-tuple-element.16.kn_ref, ...), custom_call_target="tpu_custom_call" | custom-call | flops 1200000000 | bytes 20000000 | tf_op jit(solution)/shard_map/attend/pallas_call | solution.py:153
  106.4 0.0 all-gather.4.cloned.1.call-done.wo_ref
  106.4 0.7 broadcast_in_dim.111.valid_ref
  107.2 68.9 %tail.1 = (bf16[7,128,256]{2,1,0:T(8,128)(2,1)}, bf16[8,128,256]{2,1,0:T(8,128)(2,1)}) custom-call(bf16[8,112,256]{2,1,0:T(8,128)(2,1)} %get-tuple-element.19.ctx_ref, bf16[7,128,1024]{2,1,0:T(8,128)(2,1)} %get-tuple-element.20.in_ref, bf16[1024,1024]{1,0:T(8,128)(2,1)} %all-gather.4.cloned.1.call-done.wo_ref, f32[1,1024]{1,0:T(1,128)} %bitcast.68, ...), custom_call_target="tpu_custom_call" | custom-call | flops 4000000000 | bytes 10000000 | tf_op jit(solution)/shard_map/tail/pallas_call | solution.py:344
  176.1 2.2 %copy.51 = bf16[128,8,256]{2,1,0:T(8,128)(2,1)} copy(bf16[128,8,256]{2,0,1:T(8,128)(2,1)} %bitcast.63) | data formatting | bytes 1048576
  178.3 0.8 copy.64
  (69 shorter events, 0.2 us)
Async XLA Ops:
  7.2 2.5 %copy-start.4 = (bf16[256,1024]{1,0:T(8,128)(2,1)S(1)}, bf16[256,1024]{1,0:T(8,128)(2,1)}, u32[]{:S(2)}) copy-start(bf16[256,1024]{1,0:T(8,128)(2,1)} %param.43) | copy-start | bytes 1572868
  7.2 70.0 %all-gather.6.cloned.1.call-start = ((), (), s32[]{:S(2)}) async-start(), calls=%async_computation.4 | async-start | bytes 1679360 | tf_op jit(solution)/shard_map/all_gather | solution.py:403
  9.7 8.5 %copy-start.19 = (s32[128]{0:T(128)S(1)}, s32[128]{0:T(128)}, u32[]{:S(2)}) copy-start(s32[128]{0:T(128)} %param.29) | copy-start | bytes 1540
  9.7 9.8 %copy-start.27 = (s32[128]{0:T(128)S(1)}, s32[128]{0:T(128)}, u32[]{:S(2)}) copy-start(s32[128]{0:T(128)} %param.28) | copy-start | bytes 1540
  9.7 10.0 %copy-start.1 = (bf16[128,56,80]{0,2,1:T(8,128)(2,1)S(1)}, bf16[128,56,80]{0,2,1:T(8,128)(2,1)}, u32[]{:S(2)}) copy-start(bf16[128,56,80]{0,2,1:T(8,128)(2,1)} %param.22) | copy-start | bytes 3440644
  10.5 32.9 %all-to-all-start.1 = ((bf16[256,4,256]{2,0,1:T(8,128)(2,1)}), bf16[256,4,256]{2,0,1:T(8,128)(2,1)}, u32[]{:S(2)}, u32[]{:S(2)}) async-start(bf16[256,4,256]{2,0,1:T(8,128)(2,1)} %bitcast.53), calls=%async_computation.1 | async-start | bytes 1048576 | tf_op jit(solution)/shard_map/all_to_all | solution.py:405
  16.9 89.6 %all-gather.4.cloned.1.call-start = ((), (), s32[]{:S(2)}) async-start(), calls=%async_computation.3 | async-start | bytes 2621440 | tf_op jit(solution)/shard_map/all_gather | solution.py:404
  18.7 1.0 copy-start.13
  18.7 7.7 %copy-start.15 = (pred[128]{0:T(512)(128)(4,1)}, pred[128]{0:T(512)(128)(4,1)S(1)}, u32[]{:S(2)}) copy-start(pred[128]{0:T(512)(128)(4,1)S(1)} %get-tuple-element.43) | copy-start | bytes 388
  20.1 3.8 %copy-start = (bf16[128,70,256]{2,0,1:T(8,128)(2,1)S(1)}, bf16[128,70,256]{2,0,1:T(8,128)(2,1)}, u32[]{:S(2)}) copy-start(bf16[128,70,256]{2,0,1:T(8,128)(2,1)} %param.25) | copy-start | bytes 13762564
  23.9 1.0 copy-start.5
  23.9 1.9 %copy-start.23 = (s32[128]{0:T(128)S(1)}, s32[128]{0:T(128)}, u32[]{:S(2)}) copy-start(s32[128]{0:T(128)} %param.30) | copy-start | bytes 1540
  23.9 3.0 %copy-start.28 = (s32[128]{0:T(128)S(1)}, s32[128]{0:T(128)}, u32[]{:S(2)}) copy-start(s32[128]{0:T(128)} %param.31) | copy-start | bytes 1540
  31.2 1.1 copy-start.14
  31.2 1.1 copy-start.16
  31.2 1.1 copy-start.24
  31.2 2.2 %copy-start.20 = (s32[256]{0:T(256)S(1)}, s32[256]{0:T(256)}, u32[]{:S(2)}) copy-start(s32[256]{0:T(256)} %and_select_fusion.1) | copy-start | bytes 3076
  31.2 2.9 %copy-start.9 = (s32[8,1,1232]{2,1,0:T(1,128)S(1)}, s32[8,1,1232]{2,1,0:T(1,128)}, u32[]{:S(2)}) copy-start(s32[8,1,1232]{2,1,0:T(1,128)} %lt.97) | copy-start | bytes 118276
  31.2 2.9 %copy-start.10 = (s32[1232]{0:T(1024)S(1)}, s32[1232]{0:T(1024)}, u32[]{:S(2)}) copy-start(s32[1232]{0:T(1024)} %ge.37) | copy-start | bytes 14788
  31.2 2.9 %copy-start.11 = (pred[1232]{0:T(1024)(128)(4,1)S(1)}, pred[1232]{0:T(1024)(128)(4,1)}, u32[]{:S(2)}) copy-start(pred[1232]{0:T(1024)(128)(4,1)} %and.141) | copy-start | bytes 3700
  31.2 2.9 %copy-start.12 = (pred[1232]{0:T(1024)(128)(4,1)S(1)}, pred[1232]{0:T(1024)(128)(4,1)}, u32[]{:S(2)}) copy-start(pred[1232]{0:T(1024)(128)(4,1)} %and.145) | copy-start | bytes 3700
  43.5 9.4 %all-to-all-start = ((bf16[8,2,4480]{2,1,0:T(2,128)(2,1)}), bf16[8,2,4480]{2,1,0:T(2,128)(2,1)S(1)}, u32[]{:S(2)}, u32[]{:S(2)}) async-start(bf16[8,2,4480]{2,1,0:T(2,128)(2,1)} %all_to_all.25), calls=%async_computation | async-start | bytes 286720 | tf_op jit(solution)/shard_map/all_to_all | solution.py:413
  49.3 7.8 %copy-start.18 = (s32[128]{0:T(128)S(1)}, s32[128]{0:T(128)}, u32[]{:S(2)}) copy-start(s32[128]{0:T(128)} %add_select_fusion.1) | copy-start | bytes 1540
  49.3 8.0 %copy-start.26 = (s32[128]{0:T(128)S(1)}, s32[128]{0:T(128)}, u32[]{:S(2)}) copy-start(s32[128]{0:T(128)} %not_convert_fusion) | copy-start | bytes 1540
  49.3 8.7 %copy-start.8 = (pred[256,256]{1,0:T(8,128)(4,1)S(1)}, pred[256,256]{1,0:T(8,128)(4,1)}, u32[]{:S(2)}) copy-start(pred[256,256]{1,0:T(8,128)(4,1)} %broadcast_compare_fusion) | copy-start | bytes 196612
  49.3 8.7 %copy-start.25 = (s32[256]{0:T(256)S(1)}, s32[256]{0:T(256)}, u32[]{:S(2)}) copy-start(s32[256]{0:T(256)} %and_select_fusion.2) | copy-start | bytes 3076
  52.9 0.7 copy-start.2
  53.5 21.0 %all-to-all-start.2 = ((bf16[16,148,256]{2,1,0:T(8,128)(2,1)}), bf16[16,148,256]{2,1,0:T(8,128)(2,1)S(1)}, u32[]{:S(2)}, u32[]{:S(2)}) async-start(bf16[16,148,256]{2,1,0:T(8,128)(2,1)} %copy.46), calls=%async_computation.2 | async-start | bytes 2490368 | tf_op jit(solution)/shard_map/all_to_all | solution.py:423
  57.1 3.1 %copy-start.3 = (bf16[8,2,4480]{2,1,0:T(2,128)(2,1)S(1)}, bf16[8,2,4480]{2,1,0:T(2,128)(2,1)}, u32[]{:S(2)}) copy-start(bf16[8,2,4480]{2,1,0:T(2,128)(2,1)} %copy-done.2) | copy-start | bytes 430084
  57.1 3.2 %copy-start.17 = (pred[128]{0:T(512)(128)(4,1)S(1)}, pred[128]{0:T(512)(128)(4,1)}, u32[]{:S(2)}) copy-start(pred[128]{0:T(512)(128)(4,1)} %copy-done.15) | copy-start | bytes 388
  61.9 12.9 %copy-start.6 = (bf16[128,8,256]{2,1,0:T(8,128)(2,1)S(1)}, bf16[128,8,256]{2,1,0:T(8,128)(2,1)}, u32[]{:S(2)}) copy-start(bf16[128,8,256]{2,1,0:T(8,128)(2,1)} %param.27) | copy-start | bytes 1572868
  77.1 10.8 %copy-start.22 = (bf16[128]{0:T(256)(128)(2,1)S(1)}, bf16[128]{0:T(256)(128)(2,1)}, u32[]{:S(2)}) copy-start(bf16[128]{0:T(256)(128)(2,1)} %get-tuple-element.42) | copy-start | bytes 772
  88.7 17.8 %copy-start.21 = (f32[128]{0:T(128)S(1)}, f32[128]{0:T(128)}, u32[]{:S(2)}) copy-start(f32[128]{0:T(128)} %get-tuple-element.47) | copy-start | bytes 1540
  176.1 2.2 %copy-start.7 = (bf16[7,128,256]{2,1,0:T(8,128)(2,1)S(1)}, bf16[7,128,256]{2,1,0:T(8,128)(2,1)}, u32[]{:S(2)}) copy-start(bf16[7,128,256]{2,1,0:T(8,128)(2,1)} %get-tuple-element.22) | copy-start | bytes 1376260
Sparse Core Ops, SparseCore 0:
  10.2 43.1 all-gather.5
  54.9 45.0 all-gather.3

commit v2 on v1

--- a/solution.py
+++ b/solution.py
@@ -6,6 +6,7 @@
 from jax import lax
 from jax.experimental import pallas as pl
 from jax.experimental.pallas import tpu as pltpu
+import numpy as np
 from jax.sharding import PartitionSpec as P
 
 KERNEL = 9
@@ -36,7 +37,7 @@
 
 
 def send_slots(new_slot, own_index, peer_count, stream_count):
-    target = new_slot // stream_count
+    target = lax.div(new_slot, stream_count)
     leaving = target != own_index
     index = jnp.arange(stream_count, dtype=jnp.int32)
     earlier = (target[None, :] == target[:, None]) & (index[None, :] < index[:, None])
@@ -47,7 +48,7 @@
 
 def arrival_slots(old_slot, own_index, slots):
     stream_count = old_slot.shape[0]
-    source = old_slot // stream_count
+    source = lax.div(old_slot, stream_count)
     staying = source == own_index
     earlier = (source[None, :] == source[:, None]) & (old_slot[None, :] < old_slot[:, None])
     position = jnp.sum(earlier.astype(jnp.int32), axis=1)
@@ -97,6 +98,7 @@
         out_shape=[jax.ShapeDtypeStruct((frames, streams, width), BF)]
         + [jax.ShapeDtypeStruct((frames, streams, local), BF)] * 3,
         compiler_params=pltpu.CompilerParams(vmem_limit_bytes=VMEM_LIMIT),
+        cost_estimate=pl.CostEstimate(flops=2600000000, bytes_accessed=25000000, transcendentals=1000),
         name="project",
     )(x, sw, gain, wq, wk, wv)
 
@@ -290,7 +292,7 @@
         here = pl.ds(pl.multiple_of(chunk * GROUP, GROUP), GROUP)
         total = jnp.zeros((rows, local), F32)
         for g in range(parts):
-            share = mm(act_all[g, chunk], wc_ref[g * local : (g + 1) * local])
+            share = mm(act_all[g, chunk], wc_ref[lax.rem(me + parts - g, parts)])
             total = total + share.astype(BF).astype(F32)
         total = (total + middle_own[chunk].astype(F32)).reshape(FRAMES, GROUP, local)
         valid = valid_ref[here, :]
@@ -402,7 +404,15 @@
     bias_rows = jnp.broadcast_to(sub_bias[None], (16, local))
     sub_full = lax.all_gather(jnp.concatenate([sub_weight, bias_rows], axis=0), "enc")
     attn_full = lax.all_gather(w_attn_out, "enc", tiled=True)
-    conv_cols = lax.all_to_all(w_conv_out, "enc", split_axis=1, concat_axis=0, tiled=True)
+    parts = lax.axis_size("enc")
+    member = lax.axis_index("enc")
+    conv_cols = []
+    for shift in range(parts):
+        piece = lax.dynamic_slice_in_dim(w_conv_out, lax.rem(member + shift, parts) * local, local, 1)
+        if shift:
+            piece = lax.ppermute(piece, "enc", [(m, (m + shift) % parts) for m in range(parts)])
+        conv_cols.append(piece)
+    conv_cols = jnp.stack(conv_cols)
 
     leaving = send_slots(new_slot, own_index, peer_count, streams).astype(BF)
     arrival, staying = arrival_slots(old_slot, own_index, slots)
@@ -419,8 +429,12 @@
     conv = conv_cache.transpose(1, 0, 2)
     choose = lambda a: jnp.einsum("rs,jsc->rjc", leaving, a, preferred_element_type=F32).astype(BF)
     bundle = jnp.concatenate([choose(keys), choose(values), choose(conv)], axis=1)
-    bundle, conv_cols = lax.optimization_barrier((bundle, conv_cols))
-    recv = lax.all_to_all(bundle, "front", split_axis=0, concat_axis=0, tiled=True).transpose(1, 0, 2)
+    recv = lax.all_to_all(bundle, "front", split_axis=0, concat_axis=0, tiled=True)
+    inputs, queries, key_new, value_new = project(
+        x_new, sub_full, ln1_gain[None], w_query, w_key, w_value
+    )
+    recv, queries = lax.optimization_barrier((recv, queries))
+    recv = recv.transpose(1, 0, 2)
     keys_recv, values_recv = recv[:CACHE], recv[CACHE : 2 * CACHE]
     conv_moved = jnp.einsum(
         "sr,jrc->jsc", arriving, recv[2 * CACHE :], preferred_element_type=F32
@@ -430,35 +444,32 @@
     groups = streams // GROUP
     span = max(1, 256 // slots)
     wanted = jnp.tile(arrival.reshape(groups, GROUP), (1, span))
-    spot = jnp.arange(span * slots, dtype=jnp.int32)
-    block_of = jnp.arange(span * GROUP, dtype=jnp.int32) // GROUP
-    pick = (
-        (wanted[:, :, None] == (spot % slots)[None, None, :])
-        & (block_of[:, None] == (spot // slots)[None, :])[None]
-    ).astype(BF)
+    spot = np.arange(span * slots, dtype=np.int32)
+    block_of = np.arange(span * GROUP, dtype=np.int32) // GROUP
+    slot_in = np.where(block_of[:, None] == (spot // slots)[None, :], (spot % slots)[None, :], -1)
+    pick = (wanted[:, :, None] == slot_in.astype(np.int32)[None]).astype(BF)
     has = jnp.sum((~staying).astype(jnp.int32).reshape(groups, GROUP), axis=1)
     valid_wide = jnp.broadcast_to(valid_new.astype(F32)[:, None], (streams, local))
     bits = jnp.stack([(valid_new >> b) & 1 for b in range(3)]).astype(BF)
     bits = jnp.broadcast_to(bits[:, :, None], (3, streams, local))
     stay_wide = jnp.broadcast_to(staying.astype(BF)[:, None], (streams, local))
-    position = jnp.arange(TOTAL, dtype=jnp.int32)[:, None]
-    cache_ok = (position < CACHE) & (position >= CACHE - cache_fill[None, :])
-    new_ok = (position >= CACHE) & (position - CACHE < valid_new[None, :])
-    colbias = jnp.where(cache_ok | new_ok, 0.0, masked_score).astype(F32)
-    colbias = colbias.reshape(TOTAL, groups, GROUP).transpose(1, 0, 2).reshape(groups, 1, TOTAL * GROUP)
-    row_of = jnp.arange(FRAMES * GROUP, dtype=jnp.int32) % GROUP
-    col_of = jnp.arange(TOTAL * GROUP, dtype=jnp.int32) % GROUP
-    match = jnp.where(row_of[:, None] == col_of[None, :], 0.0, masked_score).astype(F32)
-
-    inputs, queries, key_new, value_new = project(
-        x_new, sub_full, ln1_gain[None], w_query, w_key, w_value
+    col = np.arange(TOTAL * GROUP, dtype=np.int32)
+    row = np.arange(FRAMES * GROUP, dtype=np.int32)
+    least = jnp.tile((CACHE - cache_fill).reshape(groups, GROUP), (1, TOTAL))
+    most = jnp.tile((CACHE + valid_new).reshape(groups, GROUP), (1, TOTAL))
+    spread_col = (col // GROUP)[None, :]
+    colbias = jnp.where((spread_col >= least) & (spread_col < most), 0.0, masked_score)
+    colbias = colbias.astype(F32)[:, None, :]
+    match = jnp.asarray(
+        np.where((row % GROUP)[:, None] == (col % GROUP)[None, :], 0.0, masked_score).astype(np.float32)
     )
+
     context, key_out, value_out = attend(
         has, queries, key_new, value_new, keys, values, keys_recv, values_recv, pick, bits, stay_wide,
         colbias, match,
     )
     encoded, conv_out = tail(
-        lax.axis_size("enc"), context, inputs, attn_full, ln2_gain[None], w_glu_value, w_glu_gate, conv_old,
+        parts, context, inputs, attn_full, ln2_gain[None], w_glu_value, w_glu_gate, conv_old,
         bits, depth_kernel, norm_scale[None], norm_shift[None], conv_cols, valid_wide,
     )
     back = lambda a: a.transpose(1, 0, 2)

time: 187 us -> 184 us (0.984)
  other arithmetic: 12 us -> 7.57 us
  local copies, waits for them, and re-layouts: 15.7 us -> 11.6 us
  waiting for transfers between devices: 25.6 us -> 29.4 us
    all_gather x1, waiting for transfers between devices: 0.01 us -> 14.9 us  [on_device(): lax.all_gather(jnp.concatenate([sub_weight, bias_rows], axis=0), 'enc')]
    all_gather x1, waiting for transfers between devices: 0.02 us -> 14.5 us  [on_device(): attn_full = lax.all_gather(w_attn_out, 'enc', tiled=True)]
    all_to_all x1, waiting for transfers between devices: 12.7 us -> 0.01 us  [on_device(): lax.all_to_all(bundle, 'front', split_axis=0, concat_axis=0, tiled=True)]
    all_to_all x1 -> x0, waiting for transfers between devices: 8.62 us -> none  [on_device(): lax.all_to_all(w_conv_out, 'enc', split_axis=1, concat_axis=0, tiled=True)]
    all_to_all x1 -> x0, starting transfers between devices: 6.32 us -> none  [on_device(): lax.all_to_all(w_conv_out, 'enc', split_axis=1, concat_axis=0, tiled=True)]
    ppermute x0 -> x3, starting transfers between devices: none -> 5.51 us  [on_device(): lax.ppermute(piece, 'enc', [(m, (m + shift) % parts) for m in range(parts)])]
    all_to_all x1, waiting for transfers between devices: 3.54 us -> 0.01 us  [on_device(): lax.all_to_all(x_send, 'front', split_axis=0, concat_axis=0, tiled=True)]
    select_n x7 -> x1, other arithmetic: 2.76 us -> 0.68 us  [on_device(): jnp.where((spread_col >= least) & (spread_col < most), 0.0, masked_score)]
  transfers between devices with their start and end apart: 5 -> 7, of which waited for: 3 -> 2; matrix products, arithmetic and copies ran while one was open for 15% -> 11% of each run, Pallas kernels for 15% -> 15%
where the time goes in v2:
time: 184 us; the launch traced here: 183 us
  Pallas kernels  97 us (53%)
  waiting for transfers between devices  29.4 us (16%)
  starting transfers between devices  15.2 us (8%)
  between operations  14.3 us (8%)
  local copies, waits for them, and re-layouts  11.6 us (6%)
  matrix products  8.39 us (5%)
  other arithmetic  7.57 us (4%)
    pallas_call x1, Pallas kernels, tail(): pl.pallas_call(functools.partial(tail_kernel, parts, chunks), in_specs=[v...  69.1 us
    pallas_call x1, Pallas kernels, attend(): pl.pallas_call(attend_kernel, grid_spec=pltpu.PrefetchScalarGridSpec(num_...  17.9 us
    all_gather x1, waiting for transfers between devices, on_device(): lax.all_gather(jnp.concatenate([sub_weight, bias_rows], axis=0), 'enc')  14.9 us
    all_gather x1, waiting for transfers between devices, on_device(): attn_full = lax.all_gather(w_attn_out, 'enc', tiled=True)  14.5 us
    pallas_call x1, Pallas kernels, project(): pl.pallas_call(project_kernel, grid=(frames,), in_specs=[pl.BlockSpec((1,...  10 us
    ppermute x3, starting transfers between devices, on_device(): lax.ppermute(piece, 'enc', [(m, (m + shift) % parts) for m in range(parts)])  5.51 us
    all_to_all x1, starting transfers between devices, on_device(): lax.all_to_all(x_send, 'front', split_axis=0, concat_axis=0, tiled=True)  5.3 us
    all_to_all x1, starting transfers between devices, on_device(): lax.all_to_all(bundle, 'front', split_axis=0, concat_axis=0, tiled=True)  4.32 us
  transfers between devices with their start and end apart: 7, of which 2 were waited for; matrix products, arithmetic and copies ran while one was open for 11% of the time, Pallas kernels for 15%

profile of v2, /device:TPU:0, one launch (start us, length us, event | category | flops | bytes accessed | tf_op | source)
XLA Modules:
  0.0 183.4 jit_solution(18050026011653419313)
XLA Ops:
  7.2 0.0 all-gather.6.cloned.1.call-start
  7.2 0.7 broadcast_in_dim.46
  7.9 1.7 pad_maximum_fusion.2
  9.6 0.0 all-gather.6.cloned.1.call-update
  9.6 0.8 fusion.24
  10.4 0.2 convert_reduce_fusion.1
  10.6 1.7 convolution_convert_fusion.1
  12.2 0.7 all_to_all.12
  13.0 5.3 %all-to-all-start.1 = ((bf16[8,2,4480]{2,1,0:T(2,128)(2,1)}), bf16[8,2,4480]{2,1,0:T(2,128)(2,1)S(1)}, u32[]{:S(2)}, u32[]{:S(2)}) async-start(bf16[8,2,4480]{2,1,0:T(2,128)(2,1)} %all_to_all.12), calls=%async_computation.1 | async-start | bytes 286720 | tf_op jit(solution)/shard_map/all_to_all | solution.py:423
  18.3 0.0 copy-start.5
  18.3 0.0 all-gather.4.cloned.1.call-start
  18.4 0.0 copy-done.2
  18.4 0.8 dynamic-slice_bitcast_fusion
  19.2 1.6 collective-permute-start
  20.7 2.6 %collective-permute-start.1 = (bf16[256,256]{1,0:T(8,128)(2,1)}, bf16[256,256]{1,0:T(8,128)(2,1)}, u32[]{:S(2)}, u32[]{:S(2)}) collective-permute-start(bf16[256,256]{1,0:T(8,128)(2,1)} %get-tuple-element.50), channel_id=1, source_target_pairs={{0,2},{1,3},{2,0},{3,1},{4,6},{5,7},{6,4},{7,5},{8,10},{9,11},{10,... | collective-permute-start | bytes 393224 | tf_op jit(solution)/shard_map/ppermute | solution.py:413
  23.3 1.3 collective-permute-start.2
  24.7 0.0 all-gather.4.cloned.1.call-update
  24.7 0.0 copy-done.3
  24.7 0.2 convolution_convert_fusion.5
  24.9 0.0 copy-done.7
  24.9 0.2 convert_reduce_fusion
  25.1 0.1 tile.29
  25.2 0.1 tile.31
  25.3 0.0 copy-done.8
  25.3 0.0 copy-done.5
  25.3 1.3 compare_convert_fusion.pick_ref
  26.7 3.1 %convolution_convert_fusion.2 = bf16[16,70,256]{2,0,1:T(8,128)(2,1)S(1)} fusion(s32[128]{0:T(128)S(1)} %compare_select_fusion.4, bf16[128,70,256]{2,0,1:T(8,128)(2,1)} %param.29), kind=kOutput, calls=%fused_computation.4 | convolution fusion | flops 73689088 | bytes 5161472 | tf_op jit(solution)/shard_map/rs,jsc->rjc/dot_general | solution.py:430
  29.8 0.5 copy-done
  30.4 0.7 convolution_convert_fusion.3
  31.1 0.2 pad_maximum_fusion
  31.2 1.4 copy.45
  32.7 0.1 reshape.160
  32.7 0.6 reduce_sum.27.has_ref
  33.4 0.1 tile.35
  33.5 0.2 tile.39
  33.7 0.1 tile.32
  33.8 0.2 tile.38
  34.0 0.0 copy-start.6
  34.0 0.0 copy-start.1
  34.0 0.0 all-to-all-done.1
  34.0 4.3 %all-to-all-start = ((bf16[16,148,256]{2,1,0:T(8,128)(2,1)}), bf16[16,148,256]{2,1,0:T(8,128)(2,1)S(1)}, u32[]{:S(2)}, u32[]{:S(2)}) async-start(bf16[16,148,256]{2,1,0:T(8,128)(2,1)} %copy.45), calls=%async_computation | async-start | bytes 2490368 | tf_op jit(solution)/shard_map/all_to_all | solution.py:432
  38.3 0.0 copy-done.6
  38.3 0.7 and_select_fusion.colbias_ref
  39.0 0.1 all_to_all.14
  39.1 0.0 copy-done.1
  39.1 1.5 fusion
  40.6 0.0 collective-permute-done
  40.6 0.0 collective-permute-done.1
  40.6 0.0 collective-permute-done.2
  40.6 1.9 %pad_maximum_fusion.1.wc_ref = bf16[4,256,256]{2,1,0:T(8,128)(2,1)} fusion(bf16[1,256,256]{2,1,0:T(8,128)(2,1)} %bitcast.22, bf16[1,256,256]{2,1,0:T(8,128)(2,1)} %bitcast.21, bf16[1,256,256]{2,1,0:T(8,128)(2,1)} %bitcast.20, bf16[1,256,256]{2,1,0:T(8,128)(2,1)S(1)} %get-tuple-element.47), kind=kLoop, calls=%fused_computation.12 | loop fusion | flops 786432 | bytes 1048576 | tf_op jit(solution)/shard_map/stack | solution.py:415
  42.5 14.9 %all-gather.6.cloned.1.call-done = bf16[2624,256]{1,0:T(8,128)(2,1)} async-done(((bf16[656,256]{1,0:T(8,128)(2,1)}), bf16[2624,256]{1,0:T(8,128)(2,1)}) %all-gather.6.cloned.1.call-update) | async-done | bytes 1343504 | tf_op jit(solution)/shard_map/all_gather | solution.py:405
  57.4 10.0 %project.1 = (bf16[7,128,1024]{2,1,0:T(8,128)(2,1)}, bf16[7,128,256]{2,1,0:T(8,128)(2,1)}, bf16[7,128,256]{2,1,0:T(8,128)(2,1)}, bf16[7,128,256]{2,1,0:T(8,128)(2,1)}) custom-call(bf16[7,640,128]{2,1,0:T(8,128)(2,1)} %bitcast.58, bf16[4,656,256]{2,1,0:T(8,128)(2,1)} %bitcast.63, f32[1,1024]{1,0:T(1,128)} %bitcast.64, bf16[1024,256]{1,0:T(8,128)(2,1)} %wq_ref.1, ...), custom_call_target="tpu_custom_call" | custom-call | flops 2600000000 | bytes 25000000 | tf_op jit(solution)/shard_map/project/pallas_call | solution.py:86
  67.4 0.0 all-to-all-done
  67.5 0.2 copy.58
  67.7 1.1 fusion.23
  68.8 0.8 broadcast_in_dim.48.bits_ref
  69.6 0.7 broadcast_in_dim.51.stay_ref
  70.3 17.9 %attend.1 = (bf16[8,112,256]{2,1,0:T(8,128)(2,1)}, bf16[70,128,256]{2,1,0:T(8,128)(2,1)}, bf16[70,128,256]{2,1,0:T(8,128)(2,1)}) custom-call(s32[8]{0:T(128)} %reduce_sum.27.has_ref, bf16[7,128,256]{2,1,0:T(8,128)(2,1)} %get-tuple-element.16.q_ref, bf16[7,128,256]{2,1,0:T(8,128)(2,1)} %get-tuple-element.17.kn_ref, ...), custom_call_target="tpu_custom_call" | custom-call | flops 1200000000 | bytes 20000000 | tf_op jit(solution)/shard_map/attend/pallas_call | solution.py:155
  88.2 1.2 fusion.2.conv_ref
  89.3 14.5 %all-gather.4.cloned.1.call-done.wo_ref = bf16[1024,1024]{1,0:T(8,128)(2,1)} async-done(((bf16[256,1024]{1,0:T(8,128)(2,1)}), bf16[1024,1024]{1,0:T(8,128)(2,1)}) %all-gather.4.cloned.1.call-update) | async-done | bytes 2097168 | tf_op jit(solution)/shard_map/all_gather | solution.py:406
  103.8 0.7 broadcast_in_dim.93.valid_ref
  104.6 69.1 %tail.1 = (bf16[7,128,256]{2,1,0:T(8,128)(2,1)}, bf16[8,128,256]{2,1,0:T(8,128)(2,1)}) custom-call(bf16[8,112,256]{2,1,0:T(8,128)(2,1)} %get-tuple-element.20.ctx_ref, bf16[7,128,1024]{2,1,0:T(8,128)(2,1)} %get-tuple-element.21.in_ref, bf16[1024,1024]{1,0:T(8,128)(2,1)} %all-gather.4.cloned.1.call-done.wo_ref, f32[1,1024]{1,0:T(1,128)} %bitcast.65, ...), custom_call_target="tpu_custom_call" | custom-call | flops 4000000000 | bytes 10000000 | tf_op jit(solution)/shard_map/tail/pallas_call | solution.py:346
  173.7 2.2 %copy.50 = bf16[128,8,256]{2,1,0:T(8,128)(2,1)} copy(bf16[128,8,256]{2,0,1:T(8,128)(2,1)} %bitcast.59) | data formatting | bytes 1048576
  175.8 0.8 copy.60
  (16 shorter events, 0.1 us)
Async XLA Ops:
  7.2 50.3 %all-gather.6.cloned.1.call-start = ((), (), s32[]{:S(2)}) async-start(), calls=%async_computation.3 | async-start | bytes 1679360 | tf_op jit(solution)/shard_map/all_gather | solution.py:405
  9.6 8.8 %copy-start.2 = (bf16[256,1024]{1,0:T(8,128)(2,1)S(1)}, bf16[256,1024]{1,0:T(8,128)(2,1)}, u32[]{:S(2)}) copy-start(bf16[256,1024]{1,0:T(8,128)(2,1)} %param.46) | copy-start | bytes 1572868
  12.2 12.5 %copy-start.3 = (bf16[128,8,256]{2,1,0:T(8,128)(2,1)S(1)}, bf16[128,8,256]{2,1,0:T(8,128)(2,1)}, u32[]{:S(2)}) copy-start(bf16[128,8,256]{2,1,0:T(8,128)(2,1)} %param.30) | copy-start | bytes 1572868
  13.0 11.9 %copy-start.7 = (s32[128]{0:T(128)S(1)}, s32[128]{0:T(128)}, u32[]{:S(2)}) copy-start(s32[128]{0:T(128)} %param.32) | copy-start | bytes 1540
  13.0 21.0 %all-to-all-start.1 = ((bf16[8,2,4480]{2,1,0:T(2,128)(2,1)}), bf16[8,2,4480]{2,1,0:T(2,128)(2,1)S(1)}, u32[]{:S(2)}, u32[]{:S(2)}) async-start(bf16[8,2,4480]{2,1,0:T(2,128)(2,1)} %all_to_all.12), calls=%async_computation.1 | async-start | bytes 286720 | tf_op jit(solution)/shard_map/all_to_all | solution.py:423
  18.3 7.0 %copy-start.8 = (s32[128]{0:T(128)S(1)}, s32[128]{0:T(128)}, u32[]{:S(2)}) copy-start(s32[128]{0:T(128)} %param.34) | copy-start | bytes 1540
  18.3 7.1 %copy-start.5 = (s32[256,256]{1,0:T(8,128)S(1)}, s32[256,256]{1,0:T(8,128)}, u32[]{:S(2)}) copy-start(s32[256,256]{1,0:T(8,128)} %constant.56) | copy-start | bytes 786436
  18.3 85.5 %all-gather.4.cloned.1.call-start = ((), (), s32[]{:S(2)}) async-start(), calls=%async_computation.2 | async-start | bytes 2621440 | tf_op jit(solution)/shard_map/all_gather | solution.py:406
  19.2 21.5 %collective-permute-start = (bf16[256,256]{1,0:T(8,128)(2,1)}, bf16[256,256]{1,0:T(8,128)(2,1)}, u32[]{:S(2)}, u32[]{:S(2)}) collective-permute-start(bf16[256,256]{1,0:T(8,128)(2,1)} %get-tuple-element.48), channel_id=1, source_target_pairs={{0,1},{1,2},{2,3},{3,0},{4,5},{5,6},{6,7},{7,4},{8,9},{9,10},{10,1... | collective-permute-start | bytes 393224 | tf_op jit(solution)/shard_map/ppermute | solution.py:413
  20.7 19.9 %collective-permute-start.1 = (bf16[256,256]{1,0:T(8,128)(2,1)}, bf16[256,256]{1,0:T(8,128)(2,1)}, u32[]{:S(2)}, u32[]{:S(2)}) collective-permute-start(bf16[256,256]{1,0:T(8,128)(2,1)} %get-tuple-element.50), channel_id=1, source_target_pairs={{0,2},{1,3},{2,0},{3,1},{4,6},{5,7},{6,4},{7,5},{8,10},{9,11},{10,... | collective-permute-start | bytes 393224 | tf_op jit(solution)/shard_map/ppermute | solution.py:413
  23.3 17.3 %collective-permute-start.2 = (bf16[256,256]{1,0:T(8,128)(2,1)S(1)}, bf16[256,256]{1,0:T(8,128)(2,1)}, u32[]{:S(2)}, u32[]{:S(2)}) collective-permute-start(bf16[256,256]{1,0:T(8,128)(2,1)S(1)} %get-tuple-element.49), channel_id=1, source_target_pairs={{0,3},{1,0},{2,1},{3,2},{4,7},{5,4},{6,5},{7,6},{8,11},{9,8},{10,9... | collective-permute-start | bytes 393224 | tf_op jit(solution)/shard_map/ppermute | solution.py:413
  26.7 3.7 %copy-start = (bf16[128,70,256]{2,0,1:T(8,128)(2,1)S(1)}, bf16[128,70,256]{2,0,1:T(8,128)(2,1)}, u32[]{:S(2)}) copy-start(bf16[128,70,256]{2,0,1:T(8,128)(2,1)} %param.28) | copy-start | bytes 13762564
  34.0 4.4 %copy-start.6 = (s32[1232]{0:T(1024)S(1)}, s32[1232]{0:T(1024)}, u32[]{:S(2)}) copy-start(s32[1232]{0:T(1024)} %constant.57) | copy-start | bytes 14788
  34.0 5.1 %copy-start.1 = (bf16[128,56,80]{0,2,1:T(8,128)(2,1)S(1)}, bf16[128,56,80]{0,2,1:T(8,128)(2,1)}, u32[]{:S(2)}) copy-start(bf16[128,56,80]{0,2,1:T(8,128)(2,1)} %param.25) | copy-start | bytes 3440644
  34.0 33.4 %all-to-all-start = ((bf16[16,148,256]{2,1,0:T(8,128)(2,1)}), bf16[16,148,256]{2,1,0:T(8,128)(2,1)S(1)}, u32[]{:S(2)}, u32[]{:S(2)}) async-start(bf16[16,148,256]{2,1,0:T(8,128)(2,1)} %copy.45), calls=%async_computation | async-start | bytes 2490368 | tf_op jit(solution)/shard_map/all_to_all | solution.py:432
  173.6 2.2 %copy-start.4 = (bf16[7,128,256]{2,1,0:T(8,128)(2,1)S(1)}, bf16[7,128,256]{2,1,0:T(8,128)(2,1)}, u32[]{:S(2)}) copy-start(bf16[7,128,256]{2,1,0:T(8,128)(2,1)} %get-tuple-element.22) | copy-start | bytes 1376260
Sparse Core Ops, SparseCore 0:
  10.1 47.2 all-gather.5
  59.0 44.7 all-gather.3

commit v3 on v2

--- a/solution.py
+++ b/solution.py
@@ -401,9 +401,16 @@
     slots = peer_count * CAP
     mels = spectra.shape[2]
 
-    bias_rows = jnp.broadcast_to(sub_bias[None], (16, local))
-    sub_full = lax.all_gather(jnp.concatenate([sub_weight, bias_rows], axis=0), "enc")
-    attn_full = lax.all_gather(w_attn_out, "enc", tiled=True)
+    def gather_shared(weight):
+        share = weight.shape[0] // peer_count
+        own = lax.dynamic_slice_in_dim(weight, own_index * share, share, 0)
+        return lax.all_gather(own, ("enc", "front"), tiled=True)
+
+    bias_rows = -sub_weight.shape[0] % (8 * peer_count) or 8 * peer_count
+    bias_rows = jnp.broadcast_to(sub_bias[None], (bias_rows, local))
+    sub_full = gather_shared(jnp.concatenate([sub_weight, bias_rows], axis=0))
+    sub_full = sub_full.reshape(lax.axis_size("enc"), -1, local)
+    attn_full = gather_shared(w_attn_out)
     parts = lax.axis_size("enc")
     member = lax.axis_index("enc")
     conv_cols = []

time: 184 us -> 212 us (1.15)
  waiting for transfers between devices: 29.4 us -> 57 us
    all_gather x2, waiting for transfers between devices: 29.4 us -> 56.9 us  [gather_shared(): return lax.all_gather(own, ('enc', 'front'), tiled=True)]
  transfers between devices with their start and end apart: 7 -> 7, of which waited for: 2 -> 2; matrix products, arithmetic and copies ran while one was open for 11% -> 10% of each run, Pallas kernels for 15% -> 13%
where the time goes in v3:
time: 212 us; the launch traced here: 211 us
  Pallas kernels  96.9 us (46%)
  waiting for transfers between devices  57 us (27%)
  starting transfers between devices  15.2 us (7%)
  between operations  14.3 us (7%)
  local copies, waits for them, and re-layouts  12.3 us (6%)
  matrix products  8.39 us (4%)
  other arithmetic  7.44 us (4%)
    pallas_call x1, Pallas kernels, tail(): pl.pallas_call(functools.partial(tail_kernel, parts, chunks), in_specs=[v...  69.1 us
    all_gather x2, waiting for transfers between devices, gather_shared(): return lax.all_gather(own, ('enc', 'front'), tiled=True)  56.9 us
    pallas_call x1, Pallas kernels, attend(): pl.pallas_call(attend_kernel, grid_spec=pltpu.PrefetchScalarGridSpec(num_...  17.7 us
    pallas_call x1, Pallas kernels, project(): pl.pallas_call(project_kernel, grid=(frames,), in_specs=[pl.BlockSpec((1,...  10 us
    ppermute x3, starting transfers between devices, on_device(): lax.ppermute(piece, 'enc', [(m, (m + shift) % parts) for m in range(parts)])  5.51 us
    all_to_all x1, starting transfers between devices, on_device(): lax.all_to_all(x_send, 'front', split_axis=0, concat_axis=0, tiled=True)  5.3 us
    all_to_all x1, starting transfers between devices, on_device(): lax.all_to_all(bundle, 'front', split_axis=0, concat_axis=0, tiled=True)  4.28 us
  transfers between devices with their start and end apart: 7, of which 2 were waited for; matrix products, arithmetic and copies ran while one was open for 10% of the time, Pallas kernels for 13%

profile of v3, /device:TPU:0, one launch (start us, length us, event | category | flops | bytes accessed | tf_op | source)
XLA Modules:
  0.0 211.5 jit_solution(17150936539997752044)
XLA Ops:
  7.2 0.0 copy-start
  7.2 0.0 all-gather.3.cloned.1.call-start
  7.2 0.7 broadcast_in_dim.46
  7.9 1.5 fusion.6
  9.5 0.0 all-gather.3.cloned.1.call-update
  9.5 0.7 fusion.25
  10.2 0.2 convert_reduce_fusion.1
  10.4 1.7 convolution_convert_fusion.1
  12.1 0.0 copy-start.10
  12.1 0.0 copy-start.4
  12.1 0.7 all_to_all.12
  12.8 5.3 %all-to-all-start.1 = ((bf16[8,2,4480]{2,1,0:T(2,128)(2,1)}), bf16[8,2,4480]{2,1,0:T(2,128)(2,1)S(1)}, u32[]{:S(2)}, u32[]{:S(2)}) async-start(bf16[8,2,4480]{2,1,0:T(2,128)(2,1)} %all_to_all.12), calls=%async_computation.1 | async-start | bytes 286720 | tf_op jit(solution)/shard_map/all_to_all | solution.py:430
  18.1 0.0 all-gather.5.cloned.1.call-start
  18.2 0.0 copy-done.3
  18.2 0.8 dynamic-slice_bitcast_fusion
  19.0 1.6 collective-permute-start
  20.6 2.6 %collective-permute-start.1 = (bf16[256,256]{1,0:T(8,128)(2,1)}, bf16[256,256]{1,0:T(8,128)(2,1)}, u32[]{:S(2)}, u32[]{:S(2)}) collective-permute-start(bf16[256,256]{1,0:T(8,128)(2,1)} %get-tuple-element.50), channel_id=1, source_target_pairs={{0,2},{1,3},{2,0},{3,1},{4,6},{5,7},{6,4},{7,5},{8,10},{9,11},{10,... | collective-permute-start | bytes 393224 | tf_op jit(solution)/shard_map/ppermute | solution.py:420
  23.1 1.3 collective-permute-start.2
  24.5 0.0 copy-done
  24.5 0.6 constant_dynamic-slice_fusion.3
  25.1 0.0 all-gather.5.cloned.1.call-update
  25.2 0.0 copy-done.9
  25.2 0.2 convert_reduce_fusion
  25.4 0.1 tile.29
  25.5 0.1 tile.31
  25.6 0.2 convolution_convert_fusion.5
  25.8 1.3 compare_convert_fusion.pick_ref
  27.1 3.1 %convolution_convert_fusion.2 = bf16[16,70,256]{2,0,1:T(8,128)(2,1)S(1)} fusion(s32[128]{0:T(128)S(1)} %compare_select_fusion.4, bf16[128,70,256]{2,0,1:T(8,128)(2,1)} %param.29), kind=kOutput, calls=%fused_computation.4 | convolution fusion | flops 73689088 | bytes 5161472 | tf_op jit(solution)/shard_map/rs,jsc->rjc/dot_general | solution.py:437
  30.3 0.5 copy-done.1
  30.8 0.7 convolution_convert_fusion.3
  31.5 0.2 pad_maximum_fusion
  31.7 1.4 copy.45
  33.1 0.1 reshape.164
  33.2 0.7 reduce_sum.27.has_ref
  33.9 0.1 tile.35
  34.0 0.2 tile.39
  34.2 0.1 tile.32
  34.3 0.2 tile.38
  34.5 0.0 copy-start.8
  34.5 0.0 copy-start.2
  34.5 0.0 all-to-all-done.1
  34.5 4.3 %all-to-all-start = ((bf16[16,148,256]{2,1,0:T(8,128)(2,1)}), bf16[16,148,256]{2,1,0:T(8,128)(2,1)S(1)}, u32[]{:S(2)}, u32[]{:S(2)}) async-start(bf16[16,148,256]{2,1,0:T(8,128)(2,1)} %copy.45), calls=%async_computation | async-start | bytes 2490368 | tf_op jit(solution)/shard_map/all_to_all | solution.py:439
  38.8 0.0 copy-done.8
  38.8 0.7 and_select_fusion.colbias_ref
  39.5 0.1 all_to_all.14
  39.6 1.5 fusion
  41.1 0.0 collective-permute-done
  41.1 0.0 collective-permute-done.1
  41.1 0.0 collective-permute-done.2
  41.1 1.9 pad_maximum_fusion.1.wc_ref
  43.0 30.5 %all-gather.3.cloned.1.call-done = bf16[2816,256]{1,0:T(8,128)(2,1)} async-done(((bf16[88,256]{1,0:T(8,128)(2,1)}), bf16[2816,256]{1,0:T(8,128)(2,1)}) %all-gather.3.cloned.1.call-update) | async-done | bytes 1441808 | tf_op jit(solution)/shard_map/all_gather | solution.py:407
  73.5 10.0 %project.1 = (bf16[7,128,1024]{2,1,0:T(8,128)(2,1)}, bf16[7,128,256]{2,1,0:T(8,128)(2,1)}, bf16[7,128,256]{2,1,0:T(8,128)(2,1)}, bf16[7,128,256]{2,1,0:T(8,128)(2,1)}) custom-call(bf16[7,640,128]{2,1,0:T(8,128)(2,1)} %bitcast.58, bf16[4,704,256]{2,1,0:T(8,128)(2,1)} %bitcast.63, f32[1,1024]{1,0:T(1,128)} %bitcast.64, bf16[1024,256]{1,0:T(8,128)(2,1)} %wq_ref.1, ...), custom_call_target="tpu_custom_call" | custom-call | flops 2600000000 | bytes 25000000 | tf_op jit(solution)/shard_map/project/pallas_call | solution.py:86
  83.5 0.0 all-to-all-done
  83.5 0.2 copy.58
  83.8 1.1 fusion.24
  84.9 0.8 broadcast_in_dim.48.bits_ref
  85.7 0.7 broadcast_in_dim.51.stay_ref
  86.4 17.7 %attend.1 = (bf16[8,112,256]{2,1,0:T(8,128)(2,1)}, bf16[70,128,256]{2,1,0:T(8,128)(2,1)}, bf16[70,128,256]{2,1,0:T(8,128)(2,1)}) custom-call(s32[8]{0:T(128)} %reduce_sum.27.has_ref, bf16[7,128,256]{2,1,0:T(8,128)(2,1)} %get-tuple-element.16.q_ref, bf16[7,128,256]{2,1,0:T(8,128)(2,1)} %get-tuple-element.17.kn_ref, ...), custom_call_target="tpu_custom_call" | custom-call | flops 1200000000 | bytes 20000000 | tf_op jit(solution)/shard_map/attend/pallas_call | solution.py:155
  104.1 1.2 fusion.2.conv_ref
  105.3 26.5 %all-gather.5.cloned.1.call-done.wo_ref = bf16[1024,1024]{1,0:T(8,128)(2,1)} async-done(((bf16[32,1024]{1,0:T(8,128)(2,1)}), bf16[1024,1024]{1,0:T(8,128)(2,1)}) %all-gather.5.cloned.1.call-update) | async-done | bytes 2097168 | tf_op jit(solution)/shard_map/all_gather | solution.py:407
  131.8 0.7 broadcast_in_dim.93.valid_ref
  132.5 69.1 %tail.1 = (bf16[7,128,256]{2,1,0:T(8,128)(2,1)}, bf16[8,128,256]{2,1,0:T(8,128)(2,1)}) custom-call(bf16[8,112,256]{2,1,0:T(8,128)(2,1)} %get-tuple-element.20.ctx_ref, bf16[7,128,1024]{2,1,0:T(8,128)(2,1)} %get-tuple-element.21.in_ref, bf16[1024,1024]{1,0:T(8,128)(2,1)} %all-gather.5.cloned.1.call-done.wo_ref, f32[1,1024]{1,0:T(1,128)} %bitcast.65, ...), custom_call_target="tpu_custom_call" | custom-call | flops 4000000000 | bytes 10000000 | tf_op jit(solution)/shard_map/tail/pallas_call | solution.py:346
  201.7 2.2 %copy.50 = bf16[128,8,256]{2,1,0:T(8,128)(2,1)} copy(bf16[128,8,256]{2,0,1:T(8,128)(2,1)} %bitcast.59) | data formatting | bytes 1048576
  203.8 0.8 copy.60
  (21 shorter events, 0.1 us)
Async XLA Ops:
  7.2 17.3 %copy-start = (bf16[256,1024]{1,0:T(8,128)(2,1)S(1)}, bf16[256,1024]{1,0:T(8,128)(2,1)}, u32[]{:S(2)}) copy-start(bf16[256,1024]{1,0:T(8,128)(2,1)} %param.39) | copy-start | bytes 1572868
  7.2 66.3 %all-gather.3.cloned.1.call-start = ((), (), s32[]{:S(2)}) async-start(), calls=%async_computation.2 | async-start | bytes 1486848 | tf_op jit(solution)/shard_map/all_gather | solution.py:407
  7.9 10.3 %copy-start.3 = (bf16[256,1024]{1,0:T(8,128)(2,1)S(1)}, bf16[256,1024]{1,0:T(8,128)(2,1)}, u32[]{:S(2)}) copy-start(bf16[256,1024]{1,0:T(8,128)(2,1)} %param.46) | copy-start | bytes 1572868
  12.1 13.1 %copy-start.9 = (s32[128]{0:T(128)S(1)}, s32[128]{0:T(128)}, u32[]{:S(2)}) copy-start(s32[128]{0:T(128)} %param.32) | copy-start | bytes 1540
  12.1 13.5 %copy-start.10 = (s32[128]{0:T(128)S(1)}, s32[128]{0:T(128)}, u32[]{:S(2)}) copy-start(s32[128]{0:T(128)} %param.34) | copy-start | bytes 1540
  12.1 13.5 %copy-start.4 = (bf16[128,8,256]{2,1,0:T(8,128)(2,1)S(1)}, bf16[128,8,256]{2,1,0:T(8,128)(2,1)}, u32[]{:S(2)}) copy-start(bf16[128,8,256]{2,1,0:T(8,128)(2,1)} %param.30) | copy-start | bytes 1572868
  12.8 13.0 %copy-start.7 = (s32[256,256]{1,0:T(8,128)S(1)}, s32[256,256]{1,0:T(8,128)}, u32[]{:S(2)}) copy-start(s32[256,256]{1,0:T(8,128)} %constant.62) | copy-start | bytes 786436
  12.8 21.7 %all-to-all-start.1 = ((bf16[8,2,4480]{2,1,0:T(2,128)(2,1)}), bf16[8,2,4480]{2,1,0:T(2,128)(2,1)S(1)}, u32[]{:S(2)}, u32[]{:S(2)}) async-start(bf16[8,2,4480]{2,1,0:T(2,128)(2,1)} %all_to_all.12), calls=%async_computation.1 | async-start | bytes 286720 | tf_op jit(solution)/shard_map/all_to_all | solution.py:430
  18.1 113.6 %all-gather.5.cloned.1.call-start = ((), (), s32[]{:S(2)}) async-start(), calls=%async_computation.3 | async-start | bytes 2162688 | tf_op jit(solution)/shard_map/all_gather | solution.py:407
  19.0 22.1 %collective-permute-start = (bf16[256,256]{1,0:T(8,128)(2,1)}, bf16[256,256]{1,0:T(8,128)(2,1)}, u32[]{:S(2)}, u32[]{:S(2)}) collective-permute-start(bf16[256,256]{1,0:T(8,128)(2,1)} %get-tuple-element.48), channel_id=1, source_target_pairs={{0,1},{1,2},{2,3},{3,0},{4,5},{5,6},{6,7},{7,4},{8,9},{9,10},{10,1... | collective-permute-start | bytes 393224 | tf_op jit(solution)/shard_map/ppermute | solution.py:420
  20.6 20.5 %collective-permute-start.1 = (bf16[256,256]{1,0:T(8,128)(2,1)}, bf16[256,256]{1,0:T(8,128)(2,1)}, u32[]{:S(2)}, u32[]{:S(2)}) collective-permute-start(bf16[256,256]{1,0:T(8,128)(2,1)} %get-tuple-element.50), channel_id=1, source_target_pairs={{0,2},{1,3},{2,0},{3,1},{4,6},{5,7},{6,4},{7,5},{8,10},{9,11},{10,... | collective-permute-start | bytes 393224 | tf_op jit(solution)/shard_map/ppermute | solution.py:420
  23.1 18.0 %collective-permute-start.2 = (bf16[256,256]{1,0:T(8,128)(2,1)S(1)}, bf16[256,256]{1,0:T(8,128)(2,1)}, u32[]{:S(2)}, u32[]{:S(2)}) collective-permute-start(bf16[256,256]{1,0:T(8,128)(2,1)S(1)} %get-tuple-element.49), channel_id=1, source_target_pairs={{0,3},{1,0},{2,1},{3,2},{4,7},{5,4},{6,5},{7,6},{8,11},{9,8},{10,9... | collective-permute-start | bytes 393224 | tf_op jit(solution)/shard_map/ppermute | solution.py:420
  27.1 3.7 %copy-start.1 = (bf16[128,70,256]{2,0,1:T(8,128)(2,1)S(1)}, bf16[128,70,256]{2,0,1:T(8,128)(2,1)}, u32[]{:S(2)}) copy-start(bf16[128,70,256]{2,0,1:T(8,128)(2,1)} %param.28) | copy-start | bytes 13762564
  34.5 4.3 %copy-start.8 = (s32[1232]{0:T(1024)S(1)}, s32[1232]{0:T(1024)}, u32[]{:S(2)}) copy-start(s32[1232]{0:T(1024)} %constant.63) | copy-start | bytes 14788
  34.5 5.1 %copy-start.2 = (bf16[128,56,80]{0,2,1:T(8,128)(2,1)S(1)}, bf16[128,56,80]{0,2,1:T(8,128)(2,1)}, u32[]{:S(2)}) copy-start(bf16[128,56,80]{0,2,1:T(8,128)(2,1)} %param.25) | copy-start | bytes 3440644
  34.5 49.0 %all-to-all-start = ((bf16[16,148,256]{2,1,0:T(8,128)(2,1)}), bf16[16,148,256]{2,1,0:T(8,128)(2,1)S(1)}, u32[]{:S(2)}, u32[]{:S(2)}) async-start(bf16[16,148,256]{2,1,0:T(8,128)(2,1)} %copy.45), calls=%async_computation | async-start | bytes 2490368 | tf_op jit(solution)/shard_map/all_to_all | solution.py:439
  86.4 17.7 %copy-start.5 = (bf16[128,8,256]{2,1,0:T(8,128)(2,1)S(1)}, bf16[128,8,256]{2,1,0:T(8,128)(2,1)}, u32[]{:S(2)}) copy-start(bf16[128,8,256]{2,1,0:T(8,128)(2,1)} %param.30) | copy-start | bytes 1572868
  201.7 2.2 %copy-start.6 = (bf16[7,128,256]{2,1,0:T(8,128)(2,1)S(1)}, bf16[7,128,256]{2,1,0:T(8,128)(2,1)}, u32[]{:S(2)}) copy-start(bf16[7,128,256]{2,1,0:T(8,128)(2,1)} %get-tuple-element.22) | copy-start | bytes 1376260
Sparse Core Ops, SparseCore 0:
  10.8 62.6 all-gather.2
  76.4 55.3 all-gather.4
